TPU v7x, 128 devices: a whole 4x4x4 slice. The times are simulated.
128 devices in a mesh: row: 16 (over x, y), col: 8 (over z, core).
Axes of the slice: x: 4, y: 4, z: 4, core: 2. Of those that a mesh axis runs over, the one named last changes fastest.
Arguments:
- residual: bfloat16 [1024, 16, 5120], P('row', None, 'col'), may hold values from -6 to 6
- positions: int32 [1024], P('row'), may hold values from 0 to 15
- norm_gain: float32 [5120], P('col'), may hold values from 0.1 to 1.9
- w_gate: bfloat16 [5120, 16384], P('col', 'row'), may hold values from -0.078125 to 0.078125
- w_up: bfloat16 [5120, 16384], P('col', 'row'), may hold values from -0.078125 to 0.078125
- covariance: float32 [16384, 16384], P('row', 'col'), may hold values from -1 to 4, as said below
Outputs:
- factor: float32 [16384, 16384], P('row', 'col')
Inputs may be any that keep to these rules, and one draw needn't show every extreme that they name: `covariance`: symmetric positive definite in the natural order of hidden units.
All inputs are finite; a program needn't handle non-finite values.
Results may differ from a plain program's by a relative error of at most 0.0041.
Values may be sent and summed in bfloat16 or wider, within the bound.
A program may use at most 128 MiB of HBM per device.

v0:
```python
import functools

import jax
import jax.numpy as jnp
from jax import lax
from jax.sharding import Mesh
from jax.sharding import PartitionSpec as P

TILE = 64
PANEL = 256
NPANEL = 2
ROW = ("row_0", "row_1")


EPSILON = 1e-06
HIGHEST_PRECISION = lax.Precision.HIGHEST


def by_axis(array, axes):
    return functools.reduce(lax.psum, axes, array)


def copy_for_each(array, axis):
    copies = jnp.broadcast_to(array, (lax.axis_size(axis), *array.shape))
    return lax.all_to_all(copies, axis, split_axis=0, concat_axis=0, tiled=True)


def of_everyone(array, axis):
    everything = copy_for_each(array, axis)
    return jnp.sum(everything, axis=0)


def joined_along(pieces, dim):
    lengths = list(pieces.shape[1:])
    lengths[dim] *= pieces.shape[0]
    return jnp.moveaxis(pieces, 0, dim).reshape(lengths)


def gathered_copies(array, axis, dim):
    return joined_along(copy_for_each(array, axis), dim)


def shortened(array):

    def short(part):
        return part.astype(jnp.bfloat16) if part.dtype == jnp.float32 else part

    return jax.tree.map(short, array)


def broadcast(value, axis, source):
    kept = jnp.where(lax.axis_index(axis) == source, value, 0).astype(value.dtype)
    return lax.psum(kept, axis)


def trailing(left_factor, right_factor):
    return lax.dot_general(
        left_factor,
        right_factor,
        (((1,), (1,)), ((), ())),
        precision=HIGHEST_PRECISION,
        preferred_element_type=jnp.float32,
    )


def unit_scale(raw_keys, wide_hidden):
    squares = by_axis(jnp.sum(raw_keys * raw_keys, axis=1), ROW)
    return (raw_keys * lax.rsqrt(squares / wide_hidden + EPSILON)[:, None]).astype(jnp.bfloat16)


def on_device(residual, positions, norm_gain, w_gate, w_up, covariance):
    row_devices = lax.axis_size(ROW)
    col_devices = lax.axis_size("col")
    row_rank = lax.axis_index(ROW)
    col_rank = lax.axis_index("col")
    local_prompts = residual.shape[0]
    token_count = residual.shape[1]
    local_feat = residual.shape[2]
    model_width = local_feat * col_devices
    hidden_local = w_gate.shape[1]
    wide_hidden = hidden_local * row_devices
    row_count = covariance.shape[0]
    col_count = covariance.shape[1]
    tiles_here = hidden_local // TILE
    panel_tiles = PANEL // TILE
    token_iota = lax.broadcasted_iota(jnp.int32, (local_prompts, token_count), 1)
    token_mask = (token_iota == positions[:, None])[:, :, None]
    picked = jnp.where(token_mask, residual, jnp.zeros_like(residual))
    subject = jnp.sum(picked.astype(jnp.float32), axis=1)
    part_squares = jnp.sum(subject * subject, axis=1)
    total_squares = of_everyone(part_squares, "col")
    inverse_rms = lax.rsqrt(total_squares / model_width + EPSILON)
    normed = (subject * inverse_rms[:, None] * norm_gain[None, :]).astype(jnp.bfloat16)
    normed_all = gathered_copies(normed, ROW, 0)
    prompts = normed_all.shape[0]
    gate_block = jnp.dot(normed_all, w_gate, preferred_element_type=jnp.float32)
    up_block = jnp.dot(normed_all, w_up, preferred_element_type=jnp.float32)
    shared = lax.psum_scatter(
        jnp.concatenate([gate_block, up_block], axis=1), "col", scatter_dimension=0, tiled=True
    )
    unit_share = unit_scale(
        jax.nn.silu(shared[:, :hidden_local]) * shared[:, hidden_local:], wide_hidden
    )
    unit_keys = gathered_copies(unit_share, "col", 0)
    grouped = (
        unit_keys.reshape(prompts, tiles_here // row_devices, row_devices, TILE)
        .transpose(0, 2, 1, 3)
        .reshape(prompts, hidden_local)
    )
    row_keys = lax.all_to_all(grouped, ROW, split_axis=1, concat_axis=1, tiled=True)
    col_split = unit_keys.reshape(prompts, tiles_here // col_devices, col_devices, TILE)
    col_pick = lax.dynamic_index_in_dim(col_split, col_rank, axis=2, keepdims=False).reshape(
        prompts, tiles_here // col_devices * TILE
    )
    col_keys = lax.all_gather(col_pick, ROW, axis=1, tiled=True)
    keys_outer = lax.dot_general(
        row_keys, col_keys, (((0,), (0,)), ((), ())), preferred_element_type=jnp.float32
    )
    updated = covariance + keys_outer * (1.0 / prompts)
    row_pos = lax.broadcasted_iota(jnp.int32, (row_count,), 0)
    row_global = (row_pos // TILE * row_devices + row_rank) * TILE + row_pos % TILE
    col_pos = lax.broadcasted_iota(jnp.int32, (col_count,), 0)
    col_global = (col_pos // TILE * col_devices + col_rank) * TILE + col_pos % TILE
    row_groups = row_devices // col_devices
    panel_iota = lax.broadcasted_iota(jnp.int32, (1, PANEL), 1)

    def col_bounds(number):
        first_tile = number * panel_tiles
        col_start = first_tile // col_devices
        col_end = (first_tile + panel_tiles - 1) // col_devices + 1
        return (col_start * TILE, col_end * TILE)

    for number in range(NPANEL):
        begin_col, end_col = col_bounds(number)
        factor_first_tile = number * panel_tiles
        factor_col_start = factor_first_tile // col_devices
        col_tiles = (factor_first_tile + panel_tiles - 1) // col_devices + 1 - factor_col_start
        gathered = gathered_copies(updated[:, begin_col:end_col], "col", 1)
        gathered = (
            gathered.reshape(row_count, col_devices, col_tiles, TILE)
            .transpose(0, 2, 1, 3)
            .reshape(row_count, col_tiles * col_devices * TILE)
        )
        col_offset = (factor_first_tile - factor_col_start * col_devices) * TILE
        panel_rows = gathered[:, col_offset : col_offset + PANEL]
        row_start = factor_first_tile // row_devices
        row_tiles = (factor_first_tile + panel_tiles - 1) // row_devices + 1 - row_start
        diag_rows = gathered_copies(
            panel_rows[row_start * TILE : (row_start + row_tiles) * TILE].astype(jnp.bfloat16),
            ROW,
            0,
        ).astype(jnp.float32)
        diag_rows = (
            diag_rows.reshape(row_devices, row_tiles, TILE, PANEL)
            .transpose(1, 0, 2, 3)
            .reshape(row_tiles * row_devices * TILE, PANEL)
        )
        row_offset = (factor_first_tile - row_start * row_devices) * TILE
        lower_factor = jnp.linalg.cholesky(diag_rows[row_offset : row_offset + PANEL])
        solved = jax.scipy.linalg.solve_triangular(lower_factor, panel_rows.T, lower=True).T
        factor_shifted = row_global - number * PANEL
        selector = (factor_shifted[:, None] == panel_iota).astype(jnp.float32)
        from_lower = jnp.dot(
            selector, lower_factor, precision=HIGHEST_PRECISION, preferred_element_type=jnp.float32
        )
        factor_panel_factor = jnp.where((factor_shifted >= PANEL)[:, None], solved, from_lower)
        received = []
        for member in range(row_groups):
            received.append(
                broadcast(
                    shortened(factor_panel_factor), ROW, col_rank + member * col_devices
                ).astype(factor_panel_factor.dtype)
            )
        column_factor = (
            jnp.stack(received, 0)
            .reshape(row_groups, row_count // TILE, TILE, PANEL)
            .transpose(1, 0, 2, 3)
            .reshape(col_count, PANEL)
        )
        panel_factor, column_factor = (factor_panel_factor, column_factor)
        updated = updated - trailing(panel_factor, column_factor)
        place_begin_col, place_end_col = col_bounds(number)
        shifted = col_global[place_begin_col:place_end_col] - number * PANEL
        within = (shifted >= 0) & (shifted < PANEL)
        column_select = (panel_iota[0][:, None] == shifted[None, :]).astype(jnp.float32)
        values = jnp.dot(
            panel_factor,
            column_select,
            precision=HIGHEST_PRECISION,
            preferred_element_type=jnp.float32,
        )
        replaced = jnp.where(within[None, :], values, updated[:, place_begin_col:place_end_col])
        updated = updated.at[:, place_begin_col:place_end_col].set(replaced)
    lower_part = row_global[:, None] >= col_global[None, :]
    return jnp.where(lower_part, updated, 0.0)


def solution(mesh):
    torus = Mesh(mesh.devices.reshape(4, 4, mesh.shape["col"]), ("row_0", "row_1", "col"))
    placed = (P(ROW, None, "col"), P(ROW), P("col"), P("col", ROW), P("col", ROW), P(ROW, "col"))
    return jax.shard_map(
        on_device, mesh=torus, in_specs=placed, out_specs=P(ROW, "col"), check_vma=False
    )
```

profile of v0, /device:TPU:20, one launch (start us, length us, event | category | flops | bytes accessed | tf_op | source)
XLA Modules:
  0.0 688.1 jit_solution(8219200208824315445)
XLA Ops:
  10.1 5.3 all-to-all-start
  15.5 5.1 all-to-all-done
  21.6 23.3 %all_to_all.48 = bf16[16,64,640]{2,1,0:T(8,128)(2,1)S(1)} all-to-all(bf16[16,64,640]{2,1,0:T(8,128)(2,1)S(1)} %broadcast_in_dim.88), channel_id=1, replica_groups=mesh['row_0'=4,'row_1'=4,'col'=8] {'row_0','row_1'}, dimensions={0} | all-to-all | bytes 2621440 | tf_op jit(solution)/shard_map/all_to_all | solution.py:25
  52.9 52.1 %reduce-scatter.2.cloned.1.call-done = f32[128,2048]{0,1:T(8,128)} async-done(((f32[1024,2048]{0,1:T(8,128)}), f32[128,2048]{0,1:T(8,128)}) %reduce-scatter.2.cloned.1.call-update) | async-done | bytes 1048592 | tf_op jit(solution)/shard_map/reduce_scatter | solution.py:98
  106.4 8.3 %psum.42 = f32[128]{0:T(128)S(1)} all-reduce(f32[128]{0:T(128)S(1)} %get-tuple-element.67), channel_id=1, replica_groups=mesh['row_0'=4,'row_1'=4,'col'=8] {'row_0'}, use_global_device_ids=true, to_apply=%region_5.6 | all-reduce | flops 128 | bytes 1024 | tf_op jit(solution)/shard_map/psum | solution.py:20
  114.7 8.3 %psum.43 = f32[128]{0:T(128)S(1)} all-reduce(f32[128]{0:T(128)S(1)} %psum.42), channel_id=1, replica_groups=mesh['row_0'=4,'row_1'=4,'col'=8] {'row_1'}, use_global_device_ids=true, to_apply=%region_6.7 | all-reduce | flops 128 | bytes 1024 | tf_op jit(solution)/shard_map/psum | solution.py:20
  124.6 4.3 all-to-all-start.2
  129.0 27.1 %all-to-all-done.2 = bf16[8,128,1024]{1,2,0:T(8,128)(2,1)} async-done(((bf16[8,128,1024]{1,2,0:T(8,128)(2,1)}), bf16[8,128,1024]{1,2,0:T(8,128)(2,1)}, u32[]{:S(2)}, u32[]{:S(2)}) %all-to-all-start.2) | async-done | bytes 2097184 | tf_op jit(solution)/shard_map/all_to_all | solution.py:25
  165.4 36.9 %all_to_all.49 = bf16[1024,16,64]{0,2,1:T(8,128)(2,1)S(1)} all-to-all(bf16[1024,16,64]{0,2,1:T(8,128)(2,1)} %all_to_all.33), channel_id=1, replica_groups=mesh['row_0'=4,'row_1'=4,'col'=8] {'row_0','row_1'}, dimensions={1} | all-to-all | bytes 4194304 | tf_op jit(solution)/shard_map/all_to_all | solution.py:110
  202.2 25.8 %all-gather.2.cloned.1.call-done = bf16[1024,2048]{0,1:T(8,128)(2,1)} async-done(((bf16[1024,128]{0,1:T(8,128)(2,1)}), bf16[1024,2048]{0,1:T(8,128)(2,1)}) %all-gather.2.cloned.1.call-update) | async-done | bytes 4194320 | tf_op jit(solution)/shard_map/all_gather | solution.py:115
  228.0 8.2 %multiply_add_fusion = f32[1024,2048]{1,0:T(8,128)S(1)} fusion(f32[1024,2048]{1,0:T(8,128)} %param.18, bf16[1024,1024]{0,1:T(8,128)(2,1)S(1)} %bitcast.126, bf16[1024,2048]{0,1:T(8,128)(2,1)} %all-gather.2.cloned.1.call-done), kind=kOutput, calls=%fused_computation.5 | convolution fusion | flops 4299161600 | bytes 23068672 | tf_op jit(solution)/shard_map/dot_general | solution.py:116
  241.5 4.6 all-to-all-start.4
  246.2 27.1 %all-to-all-done.4 = f32[8,1024,64]{1,2,0:T(8,128)S(1)} async-done(((f32[8,1024,64]{1,2,0:T(8,128)}), f32[8,1024,64]{1,2,0:T(8,128)S(1)}, u32[]{:S(2)}, u32[]{:S(2)}) %all-to-all-start.4) | async-done | bytes 2097184 | tf_op jit(solution)/shard_map/all_to_all | solution.py:25
  274.3 7.2 %all-to-all-start.5 = ((bf16[16,64,256]{2,1,0:T(8,128)(2,1)}), bf16[16,64,256]{2,1,0:T(8,128)(2,1)}, u32[]{:S(2)}, u32[]{:S(2)}) async-start(bf16[16,64,256]{2,1,0:T(8,128)(2,1)} %broadcast_in_dim.92), calls=%async_computation.6 | async-start | bytes 1048576 | tf_op jit(solution)/shard_map/all_to_all | solution.py:25
  281.7 7.5 %all-to-all-done.5 = bf16[16,64,256]{2,1,0:T(8,128)(2,1)} async-done(((bf16[16,64,256]{2,1,0:T(8,128)(2,1)}), bf16[16,64,256]{2,1,0:T(8,128)(2,1)}, u32[]{:S(2)}, u32[]{:S(2)}) %all-to-all-start.5) | async-done | bytes 524320 | tf_op jit(solution)/shard_map/all_to_all | solution.py:25
  290.3 11.7 %cholesky.130 = f32[128,128]{1,0:T(8,128)S(1)} custom-call(f32[128,128]{1,0:T(8,128)S(1)} %cholesky.194), custom_call_target="Cholesky" | custom-call | tf_op jit(solution)/shard_map/jit(cholesky)/cholesky | solution.py:159
  302.1 9.8 %custom-call.13 = f32[1,128,128]{1,2,0:T(8,128)S(1)} custom-call(f32[1,128,128]{2,1,0:T(8,128)S(1)} %get-tuple-element.84), custom_call_target="InvertDiagBlocksLowerTriangular" | custom-call | tf_op jit(solution)/shard_map/jit(cholesky)/cholesky | solution.py:159
  312.4 11.7 %cholesky.147 = f32[128,128]{1,0:T(8,128)S(1)} custom-call(f32[128,128]{1,0:T(8,128)S(1)} %convolution_subtract_fusion.5), custom_call_target="Cholesky" | custom-call | tf_op jit(solution)/shard_map/jit(cholesky)/cholesky | solution.py:159
  326.3 4.3 while.6
  330.6 19.7 %custom-call.14 = f32[2,128,128]{1,2,0:T(8,128)S(1)} custom-call(f32[2,128,128]{2,1,0:T(8,128)S(1)} %get-tuple-element.45), custom_call_target="InvertDiagBlocksLowerTriangular" | custom-call | tf_op jit(solution)/shard_map/jit(_solve_triangular)/triangular_solve | solution.py:160
  355.7 83.6 %all-reduce.8.cloned.1.call-done = (bf16[1,16,64,256]{3,2,1,0:T(8,128)(2,1)}, bf16[1,16,64,256]{3,2,1,0:T(8,128)(2,1)}) async-done(((bf16[1,16,64,256]{3,2,1,0:T(8,128)(2,1)}, bf16[1,16,64,256]{3,2,1,0:T(8,128)(2,1)}), (bf16[1,16,64,256]{3,2,1,0:T(8,128)(2,1)}, bf16[1,16,64,256]{3,2,1,0:T(8,128)(2,1)})) %all-reduce.8.cloned.1.call-update) | async-done | bytes 1048592 | tf_op jit(solution)/shard_map/psum | solution.py:53
  440.7 9.5 %convolution_subtract_fusion.1 = f32[1024,2048]{1,0:T(8,128)S(1)} fusion(f32[1024,2048]{1,0:T(8,128)} %copy-done.4, f32[1024,256]{0,1:T(8,128)S(1)} %get-tuple-element.91, bf16[2048,256]{1,0:T(8,128)(2,1)S(1)} %bitcast.124), kind=kOutput, calls=%fused_computation.8 | convolution fusion | flops 6444548096 | bytes 18874368 | tf_op jit(solution)/shard_map/dot_general | solution.py:57
  456.3 31.7 %all_to_all.50 = f32[8,1024,64]{1,2,0:T(8,128)S(1)} all-to-all(f32[8,1024,64]{1,2,0:T(8,128)S(1)} %broadcast_in_dim.96), channel_id=1, replica_groups=mesh['row_0'=4,'row_1'=4,'col'=8] {'col'}, dimensions={0} | all-to-all | bytes 4194304 | tf_op jit(solution)/shard_map/all_to_all | solution.py:25
  489.0 7.2 %all-to-all-start.7 = ((bf16[16,64,256]{2,1,0:T(8,128)(2,1)}), bf16[16,64,256]{2,1,0:T(8,128)(2,1)}, u32[]{:S(2)}, u32[]{:S(2)}) async-start(bf16[16,64,256]{2,1,0:T(8,128)(2,1)} %broadcast_in_dim.97), calls=%async_computation.8 | async-start | bytes 1048576 | tf_op jit(solution)/shard_map/all_to_all | solution.py:25
  496.7 7.0 %all-to-all-done.7 = bf16[16,64,256]{2,1,0:T(8,128)(2,1)} async-done(((bf16[16,64,256]{2,1,0:T(8,128)(2,1)}), bf16[16,64,256]{2,1,0:T(8,128)(2,1)}, u32[]{:S(2)}, u32[]{:S(2)}) %all-to-all-start.7) | async-done | bytes 524320 | tf_op jit(solution)/shard_map/all_to_all | solution.py:25
  504.9 11.7 %cholesky.164 = f32[128,128]{1,0:T(8,128)S(1)} custom-call(f32[128,128]{1,0:T(8,128)S(1)} %cholesky.197), custom_call_target="Cholesky" | custom-call | tf_op jit(solution)/shard_map/jit(cholesky)/cholesky | solution.py:159
  516.6 9.8 %custom-call.15 = f32[1,128,128]{1,2,0:T(8,128)S(1)} custom-call(f32[1,128,128]{2,1,0:T(8,128)S(1)} %get-tuple-element.80), custom_call_target="InvertDiagBlocksLowerTriangular" | custom-call | tf_op jit(solution)/shard_map/jit(cholesky)/cholesky | solution.py:159
  526.9 11.7 %cholesky.181 = f32[128,128]{1,0:T(8,128)S(1)} custom-call(f32[128,128]{1,0:T(8,128)S(1)} %convolution_subtract_fusion.4), custom_call_target="Cholesky" | custom-call | tf_op jit(solution)/shard_map/jit(cholesky)/cholesky | solution.py:159
  545.7 19.7 %custom-call.16 = f32[2,128,128]{1,2,0:T(8,128)S(1)} custom-call(f32[2,128,128]{2,1,0:T(8,128)S(1)} %get-tuple-element.46), custom_call_target="InvertDiagBlocksLowerTriangular" | custom-call | tf_op jit(solution)/shard_map/jit(_solve_triangular)/triangular_solve | solution.py:160
  573.6 80.8 %all-reduce.6.cloned.1.call-done = (bf16[1,16,64,256]{3,2,1,0:T(8,128)(2,1)}, bf16[1,16,64,256]{3,2,1,0:T(8,128)(2,1)}) async-done(((bf16[1,16,64,256]{3,2,1,0:T(8,128)(2,1)}, bf16[1,16,64,256]{3,2,1,0:T(8,128)(2,1)}), (bf16[1,16,64,256]{3,2,1,0:T(8,128)(2,1)}, bf16[1,16,64,256]{3,2,1,0:T(8,128)(2,1)})) %all-reduce.6.cloned.1.call-update) | async-done | bytes 1048592 | tf_op jit(solution)/shard_map/psum | solution.py:53
  655.8 9.5 %convolution_subtract_fusion = f32[1024,2048]{1,0:T(8,128)S(1)} fusion(f32[1024,2048]{1,0:T(8,128)} %scatter.6, f32[1024,256]{0,1:T(8,128)S(1)} %get-tuple-element.94, bf16[2048,256]{1,0:T(8,128)(2,1)S(1)} %bitcast.125), kind=kOutput, calls=%fused_computation.7 | convolution fusion | flops 6444548096 | bytes 18874368 | tf_op jit(solution)/shard_map/dot_general | solution.py:57
  673.8 7.6 %compare_select_fusion = f32[1024,2048]{1,0:T(8,128)} fusion(f32[1024,2048]{1,0:T(8,128)} %scatter.9, s32[2048]{0:T(1024)S(1)} %fusion.41, s32[1024]{0:T(1024)S(1)} %get-tuple-element.95), kind=kLoop, calls=%fused_computation.6 | loop fusion | flops 4194304 | bytes 16789504 | tf_op jit(solution)/shard_map/jit(_where)/select_n | solution.py:195
  (124 shorter events, 81.5 us)
Async XLA Ops:
  6.5 38.3 %copy-start = (bf16[640,1024]{1,0:T(8,128)(2,1)S(1)}, bf16[640,1024]{1,0:T(8,128)(2,1)}, u32[]{:S(2)}) copy-start(bf16[640,1024]{1,0:T(8,128)(2,1)} %param.17) | copy-start | bytes 3932164
  10.1 10.5 %all-to-all-start = ((f32[8,1,64]{2,1,0:T(1,128)}), f32[8,1,64]{2,1,0:T(1,128)S(1)}, u32[]{:S(2)}, u32[]{:S(2)}) async-start(f32[8,1,64]{2,1,0:T(1,128)} %broadcast_in_dim.87), calls=%async_computation | async-start | bytes 8192 | tf_op jit(solution)/shard_map/all_to_all | solution.py:25
  15.4 89.5 %reduce-scatter.2.cloned.1.call-start = ((), (), s32[]{:S(2)}) async-start(), calls=%async_computation.9 | async-start | bytes 9437184 | tf_op jit(solution)/shard_map/reduce_scatter | solution.py:98
  44.9 1.9 copy-start.7
  124.6 31.5 %all-to-all-start.2 = ((bf16[8,128,1024]{1,2,0:T(8,128)(2,1)}), bf16[8,128,1024]{1,2,0:T(8,128)(2,1)}, u32[]{:S(2)}, u32[]{:S(2)}) async-start(bf16[8,128,1024]{1,2,0:T(8,128)(2,1)} %broadcast_in_dim.89), calls=%async_computation.3 | async-start | bytes 4194304 | tf_op jit(solution)/shard_map/all_to_all | solution.py:25
  129.0 99.0 %all-gather.2.cloned.1.call-start = ((), (), s32[]{:S(2)}) async-start(), calls=%async_computation.10 | async-start | bytes 4456448 | tf_op jit(solution)/shard_map/all_gather | solution.py:115
  236.3 3.4 copy-start.4
  241.5 31.8 %all-to-all-start.4 = ((f32[8,1024,64]{1,2,0:T(8,128)}), f32[8,1024,64]{1,2,0:T(8,128)S(1)}, u32[]{:S(2)}, u32[]{:S(2)}) async-start(f32[8,1024,64]{1,2,0:T(8,128)} %broadcast_in_dim.91), calls=%async_computation.5 | async-start | bytes 4194304 | tf_op jit(solution)/shard_map/all_to_all | solution.py:25
  274.3 14.9 %all-to-all-start.5 = ((bf16[16,64,256]{2,1,0:T(8,128)(2,1)}), bf16[16,64,256]{2,1,0:T(8,128)(2,1)}, u32[]{:S(2)}, u32[]{:S(2)}) async-start(bf16[16,64,256]{2,1,0:T(8,128)(2,1)} %broadcast_in_dim.92), calls=%async_computation.6 | async-start | bytes 1048576 | tf_op jit(solution)/shard_map/all_to_all | solution.py:25
  281.5 157.8 %all-reduce.8.cloned.1.call-start = ((), (), s32[]{:S(2)}) async-start(), calls=%async_computation.12 | async-start | bytes 2097152 | tf_op jit(solution)/shard_map/psum | solution.py:53
  450.2 3.4 copy-start.2
  455.2 0.8 copy-start.5
  489.0 14.7 %all-to-all-start.7 = ((bf16[16,64,256]{2,1,0:T(8,128)(2,1)}), bf16[16,64,256]{2,1,0:T(8,128)(2,1)}, u32[]{:S(2)}, u32[]{:S(2)}) async-start(bf16[16,64,256]{2,1,0:T(8,128)(2,1)} %broadcast_in_dim.97), calls=%async_computation.8 | async-start | bytes 1048576 | tf_op jit(solution)/shard_map/all_to_all | solution.py:25
  496.2 158.2 %all-reduce.6.cloned.1.call-start = ((), (), s32[]{:S(2)}) async-start(), calls=%async_computation.11 | async-start | bytes 2097152 | tf_op jit(solution)/shard_map/psum | solution.py:53
  566.6 3.6 copy-start.6
  665.3 3.4 copy-start.3
  673.8 7.6 %copy-start.1 = (bf16[640,1024]{1,0:T(8,128)(2,1)S(1)}, bf16[640,1024]{1,0:T(8,128)(2,1)}, u32[]{:S(2)}) copy-start(bf16[640,1024]{1,0:T(8,128)(2,1)} %param.17) | copy-start | bytes 3932164
Sparse Core Ops, SparseCore 0:
  53.0 51.9 reduce-scatter.1
  163.2 64.7 all-gather.1
  355.2 84.1 all-reduce.7
  570.3 84.1 all-reduce.5
where the time goes:
time: 700 us; the launch traced here: 688 us
  waiting for transfers between devices  316 us (45%)
  other arithmetic  129 us (18%)
  blocking collectives  108 us (15%)
  local copies, waits for them, and re-layouts  48.1 us (7%)
  matrix products  40.5 us (6%)
  starting transfers between devices  29.3 us (4%)
  between operations  16.4 us (2%)
    psum x2, waiting for transfers between devices, broadcast(): return lax.psum(kept, axis)  164 us
    all_to_all x5, waiting for transfers between devices, copy_for_each(): return lax.all_to_all(copies, axis, split_axis=0, concat_axis=0, tiled=True)  73.9 us
    another operation x13, other arithmetic, on_device(): lower_factor = jnp.linalg.cholesky(diag_rows[row_offset:row_offset + PANEL])  68.7 us
    all_to_all x2, blocking collectives, copy_for_each(): return lax.all_to_all(copies, axis, split_axis=0, concat_axis=0, tiled=True)  55 us
    reduce_scatter x1, waiting for transfers between devices, on_device(): lax.psum_scatter(jnp.concatenate([gate_block, up_block], axis=1), 'col',...  52.1 us
    another operation x5, other arithmetic, on_device(): jax.scipy.linalg.solve_triangular(lower_factor, panel_rows.T, lower=True)  39.4 us
    all_to_all x1, blocking collectives, on_device(): lax.all_to_all(grouped, ROW, split_axis=1, concat_axis=1, tiled=True)  36.9 us
    all_to_all x5, starting transfers between devices, copy_for_each(): return lax.all_to_all(copies, axis, split_axis=0, concat_axis=0, tiled=True)  28.7 us
  transfers between devices with their start and end apart: 9, of which 9 were waited for; matrix products, arithmetic and copies ran while one was open for 1% of the time, Pallas kernels for 0%

commit v1 on v0

v1 whole, which is shorter than its diff:
```python
import functools

import jax
import jax.numpy as jnp
from jax import lax
from jax.experimental import pallas as pl
from jax.experimental.pallas import tpu as pltpu
from jax.sharding import Mesh
from jax.sharding import PartitionSpec as P

MESH = pl.DeviceIdType.MESH
BF16 = jnp.bfloat16
F32 = jnp.float32
EPSILON = 1e-06
HIDDEN = 16384
WIDTH = 5120
PROMPTS = 1024
VMEM_LIMIT = 60 * 1024 * 1024
BASE = 16


def here():
    return tuple(lax.axis_index(name) for name in ("x", "y", "z", "k"))


def moved(position, axis, step):
    place = list(position)
    size = 2 if axis == 3 else 4
    place[axis] = lax.rem(place[axis] + (step % size), size)
    return tuple(place)


def remote(src, dst, send, recv, target):
    return pltpu.make_async_remote_copy(
        src_ref=src, dst_ref=dst, send_sem=send, recv_sem=recv, device_id=target, device_id_type=MESH
    )


def greet(targets):
    barrier = pltpu.get_barrier_semaphore()
    for target in targets:
        pl.semaphore_signal(barrier, inc=1, device_id=target, device_id_type=MESH)
    pl.semaphore_wait(barrier, len(targets))


def when(condition, action):
    if condition is None:
        action()
    else:
        pl.when(condition)(action)


class PlaneGather:
    ORDER = (0, -1, 1, 2)

    def __init__(self, buf, rows, send, recv, pos, only=None):
        self.buf, self.rows, self.send, self.recv, self.pos, self.only = buf, rows, send, recv, pos, only

    def block(self, half, first, second):
        x, y = self.pos[0], self.pos[1]
        dx, dy = (second, first) if half == 0 else (first, second)
        return lax.rem(x + dx % 4, 4) * 4 + lax.rem(y + dy % 4, 4)

    def piece(self, half, first, second, part=None):
        size = self.rows // 2
        start = half * size
        if part is not None:
            size //= 2
            start += part * size
        return self.buf.at[self.block(half, first, second), pl.ds(start, size)]

    def copy(self, half, kind, first, second, axis, step, part=None):
        axis = axis if half == 0 else 1 - axis
        ref = self.piece(half, first, second, part)
        return remote(ref, ref, self.send.at[half, kind], self.recv.at[half, kind], moved(self.pos, axis, step))

    def sent(self):
        return {
            0: (0, 0, 1, 1, None), 1: (0, 0, 1, -1, None),
            2: (-1, 0, 1, 1, 0), 3: (1, 0, 1, -1, 1),
            4: (0, 0, 0, 1, None), 5: (-1, 0, 0, 1, None), 6: (1, 0, 0, 1, None), 7: (2, 0, 0, 1, None),
            8: (0, 0, 0, -1, None), 9: (-1, 0, 0, -1, None), 10: (1, 0, 0, -1, None), 11: (2, 0, 0, -1, None),
            12: (0, -1, 0, 1, None), 13: (-1, -1, 0, 1, None), 14: (1, 1, 0, -1, None), 15: (2, 1, 0, -1, None),
        }

    def got(self):
        return {
            0: (-1, 0, None), 1: (1, 0, None), 2: (2, 0, 0), 3: (2, 0, 1),
            4: (0, -1, None), 5: (-1, -1, None), 6: (1, -1, None), 7: (2, -1, None),
            8: (0, 1, None), 9: (-1, 1, None), 10: (1, 1, None), 11: (2, 1, None),
            12: (0, 2, None), 13: (-1, 2, None), 14: (1, 2, None), 15: (2, 2, None),
        }

    def go(self, half, kind):
        first, second, axis, step, part = self.sent()[kind]
        cond = None if self.only is None else self.block(half, first, second) < self.only
        when(cond, lambda: self.copy(half, kind, first, second, axis, step, part).start())

    def arrive(self, half, kind):
        first, second, part = self.got()[kind]
        cond = None if self.only is None else self.block(half, first, second) < self.only
        when(cond, lambda: self.copy(half, kind, first, second, 0, 1, part).wait_recv())

    def begin(self):
        for half in (0, 1):
            for kind in (0, 1, 4, 8):
                self.go(half, kind)

    def steps(self):
        for half in (0, 1):
            for kind, on in ((0, (2, 5, 9)), (1, (3, 6, 10))):
                self.arrive(half, kind)
                for nxt in on:
                    self.go(half, nxt)
                yield half, self.got()[kind][0], self.got()[kind][1]
        for half in (0, 1):
            self.arrive(half, 4)
            self.go(half, 12)
            yield half, 0, -1
            self.arrive(half, 8)
            yield half, 0, 1
        for half in (0, 1):
            self.arrive(half, 2)
            self.arrive(half, 3)
            self.go(half, 7)
            self.go(half, 11)
            yield half, 2, 0
        for half in (0, 1):
            for kind, nxt in ((5, 13), (10, 14), (9, None), (6, None), (11, 15), (7, None), (12, None), (13, None), (14, None), (15, None)):
                self.arrive(half, kind)
                if nxt is not None:
                    self.go(half, nxt)
                yield half, self.got()[kind][0], self.got()[kind][1]

    def finish(self):
        for half in (0, 1):
            for kind in range(16):
                first, second, axis, step, part = self.sent()[kind]
                cond = None if self.only is None else self.block(half, first, second) < self.only
                when(cond, lambda: self.copy(half, kind, first, second, axis, step, part).wait_send())


class ColumnGather:
    def __init__(self, buf, send, recv, pos):
        self.buf, self.send, self.recv, self.pos = buf, send, recv, pos

    def piece(self, dz, dk=0, part=None):
        z, k = self.pos[2], self.pos[3]
        slot = lax.rem(z + dz % 4, 4) * 2 + lax.rem(k + dk, 2)
        if part is None:
            return self.buf.at[slot]
        return self.buf.at[slot, pl.ds(32 * part, 32)]

    SENT = {0: (0, 2, 1, None), 1: (0, 2, -1, None), 2: (-1, 2, 1, 0), 3: (1, 2, -1, 1),
            4: (0, 3, 1, None), 5: (-1, 3, 1, None), 6: (1, 3, 1, None), 7: (2, 3, 1, None)}
    GOT = {0: (-1, 0, None), 1: (1, 0, None), 2: (2, 0, 0), 3: (2, 0, 1),
           4: (0, 1, None), 5: (-1, 1, None), 6: (1, 1, None), 7: (2, 1, None)}

    def go(self, kind):
        dz, axis, step, part = self.SENT[kind]
        ref = self.piece(dz, 0, part)
        remote(ref, ref, self.send.at[kind], self.recv.at[kind], moved(self.pos, axis, step)).start()

    def arrive(self, kind):
        dz, dk, part = self.GOT[kind]
        ref = self.piece(dz, dk, part)
        remote(ref, ref, self.send.at[kind], self.recv.at[kind], moved(self.pos, 2, 1)).wait_recv()

    def begin(self):
        for kind in (0, 1, 4):
            self.go(kind)

    def middle(self):
        self.arrive(0)
        self.go(2)
        self.go(5)
        self.arrive(1)
        self.go(3)
        self.go(6)

    def end(self):
        self.arrive(2)
        self.arrive(3)
        self.go(7)
        for kind in (4, 5, 6, 7):
            self.arrive(kind)

    def finish(self):
        for kind in range(8):
            dz, axis, step, part = self.SENT[kind]
            ref = self.piece(dz, 0, part)
            remote(ref, ref, self.send.at[kind], self.recv.at[kind], moved(self.pos, axis, step)).wait_send()


def column_peers(pos):
    peers = []
    for dz in range(4):
        for dk in range(2):
            if dz or dk:
                peers.append(moved(moved(pos, 2, dz), 3, dk))
    return peers


def to_all_columns(buf, send, recv, pos):
    copies = []
    mine = pos[2] * 2 + pos[3]
    number = 0
    for dz in range(4):
        for dk in range(2):
            if dz == 0 and dk == 0:
                continue
            target = moved(moved(pos, 2, dz), 3, dk)
            out = remote(buf.at[mine], buf.at[mine], send.at[number], recv.at[number], target)
            origin = moved(moved(pos, 2, -dz), 3, -dk)
            slot = origin[2] * 2 + origin[3]
            into = remote(buf.at[slot], buf.at[slot], send.at[number], recv.at[number], target)
            copies.append((out, into))
            number += 1
    return copies


def to_axis(buf, send, recv, pos, axis):
    copies = []
    mine = pos[axis]
    for step in (1, 2, 3):
        target = moved(pos, axis, step)
        out = remote(buf.at[mine], buf.at[mine], send.at[step - 1], recv.at[step - 1], target)
        slot = moved(pos, axis, -step)[axis]
        into = remote(buf.at[slot], buf.at[slot], send.at[step - 1], recv.at[step - 1], target)
        copies.append((out, into))
    return copies


def exchange(copies):
    for out, _ in copies:
        out.start()
    for _, into in copies:
        into.wait_recv()


def keys_kernel(
    subject_ref, gain_ref, gate_ref, up_ref, keys_ref,
    xx, own_w, other_w, sel_w, squares, part, hop_out, hop_in, total, sum_y, sum_x, sum_c,
    local_sem, w_send, w_recv, sq_send, sq_recv, x_send, x_recv, sib_send, sib_recv,
    hop_send, hop_recv, sy_send, sy_recv, sx_send, sx_recv, sc_send, sc_recv,
):
    pos = here()
    x, y, z, k = pos
    sibling = moved(pos, 3, 1)
    plane = [moved(pos, axis, step) for axis in (0, 1) for step in (1, 2, 3)]
    greet(plane + column_peers(pos))

    for index, ref in enumerate((gate_ref, up_ref)):
        remote(ref, other_w.at[index], w_send.at[index], w_recv.at[index], sibling).start()
        pltpu.make_async_copy(ref, own_w.at[index], local_sem.at[index]).start()

    subject = subject_ref[...].astype(F32)
    squared = subject * subject
    folded = squared[:, 0:128]
    for group in range(1, 5):
        folded = folded + squared[:, group * 128 : (group + 1) * 128]
    col = z * 2 + k
    squares[col] = folded
    square_copies = to_all_columns(squares, sq_send, sq_recv, pos)
    exchange(square_copies)
    everyone = squares[0]
    for member in range(1, 8):
        everyone = everyone + squares[member]
    inverse_rms = lax.rsqrt(jnp.sum(everyone, axis=1, keepdims=True) / WIDTH + EPSILON)
    mine = x * 4 + y
    xx[k, mine] = (subject * inverse_rms * gain_ref[...]).astype(BF16)

    gather = PlaneGather(xx.at[k], 64, x_send, x_recv, pos)
    gather.begin()

    def to_sibling(half, kind, first, second):
        ref = gather.piece(half, first, second)
        return remote(ref, ref, sib_send.at[half, kind], sib_recv.at[half, kind], sibling)

    def from_sibling(half, kind, first, second):
        block = gather.block(half, first, second)
        ref = xx.at[1 - k, block, pl.ds(half * 32, 32)]
        return remote(ref, ref, sib_send.at[half, kind], sib_recv.at[half, kind], sibling)

    passed = []
    for half in (0, 1):
        to_sibling(half, 0, 0, 0).start()
        passed.append((half, 0, 0, 0))

    def select(source, core):
        def body(step, carry):
            for index in range(2):
                low = source[index, :, pl.ds(pl.multiple_of(step * 128, 128), 128)]
                high = source[index, :, pl.ds(pl.multiple_of(512 + step * 128, 128), 128)]

                @pl.when(k == 0)
                def _():
                    sel_w[step, pl.ds(pl.multiple_of(core * 640, 128), 640), pl.ds(index * 128, 128)] = jnp.concatenate(
                        [low[:, :64], high[:, :64]], axis=1
                    )

                @pl.when(k == 1)
                def _():
                    sel_w[step, pl.ds(pl.multiple_of(core * 640, 128), 640), pl.ds(index * 128, 128)] = jnp.concatenate(
                        [low[:, 64:], high[:, 64:]], axis=1
                    )

            return carry

        lax.fori_loop(0, 4, body, 0)

    number = [1, 1]
    for count, (half, first, second) in enumerate(gather.steps()):
        kind = number[half]
        number[half] += 1
        to_sibling(half, kind, first, second).start()
        passed.append((half, kind, first, second))
        if count == 3:
            for index, ref in enumerate((gate_ref, up_ref)):
                pltpu.make_async_copy(ref, own_w.at[index], local_sem.at[index]).wait()
            select(own_w, k)
        if count == 7:
            for index, ref in enumerate((gate_ref, up_ref)):
                remote(ref, other_w.at[index], w_send.at[index], w_recv.at[index], sibling).wait_recv()
            select(other_w, 1 - k)
    for half, kind, first, second in passed:
        from_sibling(half, kind, first, second).wait_recv()

    def product(direction, dest):
        blocks = pl.ds(direction * 8, 8)
        left = xx[0, blocks].reshape(512, 640)
        right = xx[1, blocks].reshape(512, 640)
        return jnp.dot(left, sel_w[dest, 0:640], preferred_element_type=F32) + jnp.dot(
            right, sel_w[dest, 640:1280], preferred_element_type=F32
        )

    def hop(direction, step, sub):
        target = moved(pos, 2, 1 if direction == 0 else -1)
        return remote(
            hop_out.at[direction, step, sub], hop_in.at[direction, step, sub],
            hop_send.at[direction, step, sub], hop_recv.at[direction, step, sub], target,
        )

    def dest_of(direction, step):
        return lax.rem(z + (3 - step if direction == 0 else 1 + step), 4)

    for direction in (0, 1):
        value = product(direction, dest_of(direction, 0)).astype(BF16)
        for sub in (0, 1):
            hop_out[direction, 0, sub] = value[sub * 256 : (sub + 1) * 256]
            hop(direction, 0, sub).start()
    for step in (1, 2, 3):
        for direction in (0, 1):
            part[direction, step - 1] = product(direction, dest_of(direction, step))
    for step in (1, 2, 3):
        for sub in (0, 1):
            for direction in (0, 1):
                hop(direction, step - 1, sub).wait_recv()
                value = part[direction, step - 1, sub * 256 : (sub + 1) * 256] + hop_in[direction, step - 1, sub].astype(F32)
                if step < 3:
                    hop_out[direction, step, sub] = value.astype(BF16)
                    hop(direction, step, sub).start()
                else:
                    gate, up = value[:, :128], value[:, 128:]
                    raw = gate / (1.0 + jnp.exp(-gate)) * up
                    start = direction * 512 + sub * 256
                    total[:, start : start + 256] = raw.T
    raw = total[...]
    mass = jnp.sum(raw * raw, axis=0, keepdims=True)
    sum_y[y] = jnp.broadcast_to(mass, (8, PROMPTS))
    y_copies = to_axis(sum_y, sy_send, sy_recv, pos, 1)
    exchange(y_copies)
    sum_x[x] = sum_y[0] + sum_y[1] + sum_y[2] + sum_y[3]
    x_copies = to_axis(sum_x, sx_send, sx_recv, pos, 0)
    exchange(x_copies)
    sum_c[col] = sum_x[0] + sum_x[1] + sum_x[2] + sum_x[3]
    c_copies = to_all_columns(sum_c, sc_send, sc_recv, pos)
    exchange(c_copies)
    mass = sum_c[0]
    for member in range(1, 8):
        mass = mass + sum_c[member]
    scale = lax.rsqrt(mass[0:1] / HIDDEN + EPSILON)
    keys_ref[...] = (raw * scale).astype(BF16)

    for index, ref in enumerate((gate_ref, up_ref)):
        remote(ref, other_w.at[index], w_send.at[index], w_recv.at[index], sibling).wait_send()
    for copies in (square_copies, y_copies, x_copies, c_copies):
        for out, _ in copies:
            out.wait_send()
    gather.finish()
    for half, kind, first, second in passed:
        to_sibling(half, kind, first, second).wait_send()
    for direction in (0, 1):
        for step in range(3):
            for sub in (0, 1):
                hop(direction, step, sub).wait_send()


def make_keys(subject, gain, w_gate, w_up):
    dma = pltpu.SemaphoreType.DMA
    return pl.pallas_call(
        keys_kernel,
        name="make_keys",
        out_shape=jax.ShapeDtypeStruct((128, PROMPTS), BF16),
        in_specs=[pl.BlockSpec(memory_space=pltpu.VMEM)] * 2 + [pl.BlockSpec(memory_space=pl.ANY)] * 2,
        out_specs=pl.BlockSpec(memory_space=pltpu.VMEM),
        scratch_shapes=[
            pltpu.VMEM((2, 16, 64, 640), BF16),
            pltpu.VMEM((2, 640, 1024), BF16),
            pltpu.VMEM((2, 640, 1024), BF16),
            pltpu.VMEM((4, 1280, 256), BF16),
            pltpu.VMEM((8, 64, 128), F32),
            pltpu.VMEM((2, 3, 512, 256), F32),
            pltpu.VMEM((2, 3, 2, 256, 256), BF16),
            pltpu.VMEM((2, 3, 2, 256, 256), BF16),
            pltpu.VMEM((128, PROMPTS), F32),
            pltpu.VMEM((4, 8, PROMPTS), F32),
            pltpu.VMEM((4, 8, PROMPTS), F32),
            pltpu.VMEM((8, 8, PROMPTS), F32),
            dma((2,)), dma((2,)), dma((2,)), dma((7,)), dma((7,)), dma((2, 16)), dma((2, 16)), dma((2, 16)), dma((2, 16)),
            dma((2, 3, 2)), dma((2, 3, 2)), dma((3,)), dma((3,)), dma((3,)), dma((3,)), dma((7,)), dma((7,)),
        ],
        compiler_params=pltpu.CompilerParams(collective_id=0, has_side_effects=True, vmem_limit_bytes=VMEM_LIMIT),
    )(subject, gain, w_gate, w_up)


def spread_kernel(
    keys_ref, covr_ref, covc_ref, kc, kr, k5, cr, cc, jj,
    kc_send, kc_recv, k5_send, k5_recv, cr_send, cr_recv, cc_send, cc_recv, jj_send, jj_recv,
    row_send, row_recv, local_sem,
):
    pos = here()
    x, y, z, k = pos
    sibling = moved(pos, 3, 1)
    row = x * 4 + y
    col = z * 2 + k
    plane = [moved(pos, axis, step) for axis in (0, 1) for step in (1, -1)]
    ring = [moved(pos, 2, 1), moved(pos, 2, -1), sibling]
    greet(plane + ring)

    kc[row] = keys_ref[...]
    keys = PlaneGather(kc, 128, kc_send, kc_recv, pos)
    keys.begin()

    cr[col] = covr_ref[...]
    panel_rows = ColumnGather(cr, cr_send, cr_recv, pos)
    panel_rows.begin()

    @pl.when(row < 8)
    def _():
        cc[row] = covc_ref[...]

    covs = PlaneGather(cc, 64, cc_send, cc_recv, pos, only=8)
    covs.begin()

    panel_rows.middle()
    for _ in keys.steps():
        pass
    for _ in covs.steps():
        pass
    panel_rows.end()

    k5[col] = kc[0, 0:64]
    first_keys = ColumnGather(k5, k5_send, k5_recv, pos)
    first_keys.begin()
    jj[col] = cc[:, :, 0:64].reshape(512, 64).astype(F32).T.astype(BF16)
    corner = ColumnGather(jj, jj_send, jj_recv, pos)
    corner.begin()

    source = lax.rem(row, 8)
    source_z = source // 2
    source_k = lax.rem(source, 2)
    start = pl.multiple_of(row // 8 * 64, 64)
    away = lax.rem(z + 4 - source_z, 4)
    same = k == source_k

    def wave(group, kind, step, part=None, own=False):
        blocks = pl.ds(group * 4, 4)
        rows = pl.ds(0, 64) if part is None else pl.ds(part * 32, 32)
        dst = kr.at[blocks, rows]
        src = kc.at[blocks, pl.ds(start, 64)] if own else dst
        target = sibling if step == 0 else moved(pos, 2, step)
        return remote(src, dst, row_send.at[group, kind], row_recv.at[group, kind], target)

    def own_copy(group):
        blocks = pl.ds(group * 4, 4)
        return pltpu.make_async_copy(kc.at[blocks, pl.ds(start, 64)], kr.at[blocks], local_sem.at[group])

    @pl.when(same & (away == 0))
    def _():
        for group in range(4):
            wave(group, 0, 1, own=True).start()
            wave(group, 1, -1, own=True).start()
            wave(group, 2, 0, own=True).start()
            own_copy(group).start()

    first_keys.middle()
    corner.middle()
    first_keys.end()
    corner.end()

    @pl.when(same & (away == 1))
    def _():
        for group in range(4):
            wave(group, 0, 1).wait_recv()
            wave(group, 3, 1, part=0).start()
            wave(group, 2, 0).start()

    @pl.when(same & (away == 3))
    def _():
        for group in range(4):
            wave(group, 1, 1).wait_recv()
            wave(group, 4, -1, part=1).start()
            wave(group, 2, 0).start()

    @pl.when(same & (away == 2))
    def _():
        for group in range(4):
            wave(group, 3, 1, part=0).wait_recv()
            wave(group, 4, 1, part=1).wait_recv()
            wave(group, 2, 0).start()

    @pl.when(k != source_k)
    def _():
        for group in range(4):
            wave(group, 2, 0).wait_recv()

    @pl.when(same & (away == 0))
    def _():
        for group in range(4):
            wave(group, 0, 1, own=True).wait_send()
            wave(group, 1, -1, own=True).wait_send()
            wave(group, 2, 0, own=True).wait_send()
            own_copy(group).wait()

    @pl.when(same & (away == 1))
    def _():
        for group in range(4):
            wave(group, 3, 1, part=0).wait_send()
            wave(group, 2, 0).wait_send()

    @pl.when(same & (away == 3))
    def _():
        for group in range(4):
            wave(group, 4, -1, part=1).wait_send()
            wave(group, 2, 0).wait_send()

    @pl.when(same & (away == 2))
    def _():
        for group in range(4):
            wave(group, 2, 0).wait_send()

    keys.finish()
    covs.finish()
    panel_rows.finish()
    first_keys.finish()
    corner.finish()


def spread(keys, covr, covc):
    dma = pltpu.SemaphoreType.DMA
    return pl.pallas_call(
        spread_kernel,
        name="spread_keys",
        out_shape=(
            jax.ShapeDtypeStruct((16, 128, PROMPTS), BF16),
            jax.ShapeDtypeStruct((16, 64, PROMPTS), BF16),
            jax.ShapeDtypeStruct((8, 64, PROMPTS), BF16),
            jax.ShapeDtypeStruct((8, 64, 1024), BF16),
            jax.ShapeDtypeStruct((8, 64, 2048), BF16),
            jax.ShapeDtypeStruct((8, 64, 512), BF16),
        ),
        in_specs=[pl.BlockSpec(memory_space=pltpu.VMEM)] * 3,
        out_specs=(pl.BlockSpec(memory_space=pltpu.VMEM),) * 6,
        scratch_shapes=[
            dma((2, 16)), dma((2, 16)), dma((8,)), dma((8,)), dma((8,)), dma((8,)), dma((2, 16)), dma((2, 16)), dma((8,)), dma((8,)),
            dma((4, 5)), dma((4, 5)), dma((4,)),
        ],
        compiler_params=pltpu.CompilerParams(collective_id=1, has_side_effects=True, vmem_limit_bytes=VMEM_LIMIT),
    )(keys, covr, covc)


def split(value):
    high = value.astype(BF16)
    return high, (value - high.astype(F32)).astype(BF16)


def dot3(left, right, dims):
    lh, ll = split(left)
    rh, rl = split(right)
    dot = functools.partial(lax.dot_general, dimension_numbers=(dims, ((), ())), preferred_element_type=F32)
    return dot(lh, rh) + (dot(lh, rl) + dot(ll, rh))


def small_factor(work):
    lane = lax.broadcasted_iota(jnp.int32, (1, 128), 1)

    def body(step, carry):
        start = pl.multiple_of(step * BASE, BASE)
        rows = work[pl.ds(start, BASE), :]
        turned = pltpu.roll(rows[:, :128], lax.rem(128 - start, 128), 1)
        entry = [[jnp.broadcast_to(turned[i : i + 1, j : j + 1], (1, 128)) for j in range(i + 1)] for i in range(BASE)]
        solved = []
        for j in range(BASE):
            inverse = lax.rsqrt(entry[j][j])
            row = rows[j : j + 1, :]
            for m in range(j):
                row = row - jnp.concatenate([entry[j][m]] * 2, axis=1) * solved[m]
            solved.append(row * jnp.concatenate([inverse] * 2, axis=1))
            for i in range(j + 1, BASE):
                entry[i][j] = entry[i][j] * inverse
            for i in range(j + 1, BASE):
                for m in range(j + 1, i + 1):
                    entry[i][m] = entry[i][m] - entry[i][j] * entry[m][j]
        block = jnp.concatenate(solved, axis=0)
        work[pl.ds(start, BASE), :] = block
        later = jnp.where(lane >= start + BASE, block[:, :128], 0.0)
        lh, ll = split(later)
        rh, rl = split(block)
        left = jnp.concatenate([lh, lh, ll], axis=0)
        right = jnp.concatenate([rh, rl, rh], axis=0)
        work[...] = work[...] - lax.dot_general(left, right, (((0,), (0,)), ((), ())), preferred_element_type=F32)
        return carry

    lax.fori_loop(0, 128 // BASE, body, 0)


def factor_kernel(k5_ref, jj_ref, lower_ref, aug, work):
    keys = k5_ref[...].reshape(512, PROMPTS)
    outer = lax.dot_general(keys, keys, (((1,), (1,)), ((), ())), preferred_element_type=F32)
    aug[:, 0:512] = jj_ref[...].reshape(512, 512).astype(F32) + outer * (1.0 / PROMPTS)
    eye = (lax.broadcasted_iota(jnp.int32, (512, 512), 0) == lax.broadcasted_iota(jnp.int32, (512, 512), 1)).astype(F32)
    aug[:, 512:1024] = eye
    for number in range(4):
        lo, hi = number * 128, (number + 1) * 128
        work[:, 0:128] = aug[lo:hi, lo:hi]
        work[:, 128:256] = eye[0:128, 0:128]
        small_factor(work)
        inverse = work[:, 128:256]
        if hi < 512:
            right = dot3(inverse, aug[lo:hi, hi : 512 + lo], ((1,), (0,)))
            full = jnp.concatenate([right, inverse], axis=1)
            aug[lo:hi, hi : 512 + hi] = full
            ahead = right[:, 0 : 512 - hi]
            aug[hi:512, hi : 512 + hi] = aug[hi:512, hi : 512 + hi] - dot3(ahead, full, ((0,), (0,)))
        else:
            aug[lo:hi, 512 : 512 + lo] = dot3(inverse, aug[lo:hi, 512 : 512 + lo], ((1,), (0,)))
            aug[lo:hi, 512 + lo : 512 + hi] = inverse
    lower_ref[...] = aug[:, 512:1024]


def factor(k5, jj):
    return pl.pallas_call(
        factor_kernel,
        name="factor_corner",
        out_shape=jax.ShapeDtypeStruct((512, 512), F32),
        in_specs=[pl.BlockSpec(memory_space=pltpu.VMEM)] * 2,
        out_specs=pl.BlockSpec(memory_space=pltpu.VMEM),
        scratch_shapes=[pltpu.VMEM((512, 1024), F32), pltpu.VMEM((128, 256), F32)],
        compiler_params=pltpu.CompilerParams(vmem_limit_bytes=VMEM_LIMIT),
    )(k5, jj)


def update_kernel(cov_ref, kc_ref, kr_ref, k5_ref, cr_ref, cc_ref, inv_ref, out_ref, covb, outb, panel, in_sem, out_sem):
    x, y, z, k = here()
    row = x * 4 + y
    col = z * 2 + k
    scale = 1.0 / PROMPTS
    nt = (((1,), (1,)), ((), ()))
    nn = (((1,), (0,)), ((), ()))
    tn = (((0,), (0,)), ((), ()))
    dot = functools.partial(lax.dot_general, preferred_element_type=F32)

    def load(step):
        area = (pl.ds(step * 128, 1024 - step * 128), pl.ds(step * 256, 256))
        return pltpu.make_async_copy(cov_ref.at[area], covb.at[step % 2, pl.ds(step * 128, 1024 - step * 128)], in_sem.at[step % 2])

    def store(step):
        return pltpu.make_async_copy(outb.at[step % 2], out_ref.at[:, pl.ds(step * 256, 256)], out_sem.at[step % 2])

    load(0).start()
    load(1).start()
    inverse = inv_ref[...]
    inverse_high = inverse.astype(BF16)
    first = k5_ref[...].reshape(512, PROMPTS)
    rows = kr_ref[...].reshape(1024, PROMPTS)
    matrix_rows = cr_ref[...].reshape(512, 1024).astype(F32) + dot(first, rows, nt) * scale
    high, low = split(matrix_rows)
    panel[...] = dot(inverse_high, high, nn)
    own = inv_ref[pl.ds(pl.multiple_of(col * 64, 64), 64), :]
    own_high, own_low = split(own)
    own_panel = dot(own_high, high, nn) + (dot(own_low, high, nn) + dot(own_high, low, nn))
    panel_low = panel[...].astype(BF16)
    for step in range(8):
        top = step * 128
        height = 1024 - top
        load(step).wait()
        if step >= 2:
            store(step - 2).wait()
        cols = kc_ref[2 * step : 2 * step + 2].reshape(256, PROMPTS)
        matrix_cols = cc_ref[:, :, step * 256 : (step + 1) * 256].reshape(512, 256).astype(F32) + dot(first, cols, nt) * scale
        panel_cols = dot(inverse_high, matrix_cols.astype(BF16), nn).astype(BF16)
        value = covb[step % 2, top:1024] + dot(rows[top:], cols, nt) * scale - dot(panel_low[:, top:], panel_cols, tn)
        if step == 0:
            value = jnp.concatenate([own_panel.T, value[:, 64:]], axis=1)
        i = lax.broadcasted_iota(jnp.int32, (height, 256), 0) + top
        j = lax.broadcasted_iota(jnp.int32, (height, 256), 1) + step * 256
        row_global = (i // 64 * 16 + row) * 64 + i % 64
        col_global = (j // 64 * 8 + col) * 64 + j % 64
        outb[step % 2, top:1024] = jnp.where(row_global >= col_global, value, 0.0)
        if step:
            outb[step % 2, 0:top] = jnp.zeros((top, 256), F32)
        store(step).start()
        if step + 2 < 8:
            load(step + 2).start()
    store(6).wait()
    store(7).wait()


def update(cov, kc, kr, k5, cr, cc, inverse):
    dma = pltpu.SemaphoreType.DMA
    vmem = pl.BlockSpec(memory_space=pltpu.VMEM)
    return pl.pallas_call(
        update_kernel,
        name="update_lower",
        out_shape=jax.ShapeDtypeStruct((1024, 2048), F32),
        in_specs=[pl.BlockSpec(memory_space=pl.ANY)] + [vmem] * 6,
        out_specs=pl.BlockSpec(memory_space=pl.ANY),
        scratch_shapes=[
            pltpu.VMEM((2, 1024, 256), F32), pltpu.VMEM((2, 1024, 256), F32), pltpu.VMEM((512, 1024), F32), dma((2,)), dma((2,)),
        ],
        compiler_params=pltpu.CompilerParams(vmem_limit_bytes=VMEM_LIMIT),
    )(cov, kc, kr, k5, cr, cc, inverse)


def on_device(residual, positions, norm_gain, w_gate, w_up, covariance):
    prompts, tokens, _ = residual.shape
    token = lax.broadcasted_iota(jnp.int32, (prompts, tokens), 1)
    picked = jnp.where((token == positions[:, None])[:, :, None], residual, jnp.zeros_like(residual))
    subject = jnp.sum(picked.astype(F32), axis=1).astype(BF16)
    keys = make_keys(subject, norm_gain[None, :], w_gate, w_up)
    covr = covariance[:, 0:64].T.astype(BF16)
    covc = covariance[0:64, :].astype(BF16)
    kc, kr, k5, cr, cc, jj = spread(keys, covr, covc)
    inverse = factor(k5, jj)
    return update(covariance, kc, kr, k5, cr, cc, inverse)


def solution(mesh):
    torus = Mesh(mesh.devices.reshape(4, 4, 4, 2), ("x", "y", "z", "k"))
    row, col = ("x", "y"), ("z", "k")
    placed = (P(row, None, col), P(row), P(col), P(col, row), P(col, row), P(row, col))
    return jax.shard_map(on_device, mesh=torus, in_specs=placed, out_specs=P(row, col), check_vma=False)
```

time: 700 us -> 242 us (0.35)
  the two profiles are of different devices: /device:TPU:20 before, /device:TPU:69 now
where the time goes in v1:
time: 242 us; the launch traced here: 241 us
  Pallas kernels  231 us (95%)
  other arithmetic  7.27 us (3%)
  local copies, waits for them, and re-layouts  2.85 us (1%)
    pallas_call x1, Pallas kernels, spread(): pl.pallas_call(spread_kernel, name='spread_keys', out_shape=(jax.ShapeDty...  118 us
    pallas_call x1, Pallas kernels, make_keys(): pl.pallas_call(keys_kernel, name='make_keys', out_shape=jax.ShapeDtypeStr...  62.9 us
    pallas_call x1, Pallas kernels, factor(): pl.pallas_call(factor_kernel, name='factor_corner', out_shape=jax.ShapeDt...  29.8 us
    pallas_call x1, Pallas kernels, update(): pl.pallas_call(update_kernel, name='update_lower', out_shape=jax.ShapeDty...  20.6 us

profile of v1, /device:TPU:69, one launch (start us, length us, event | category | flops | bytes accessed | tf_op | source)
XLA Modules:
  0.0 241.3 jit_solution(5033396693800389294)
XLA Ops:
  0.0 1.3 broadcast_in_dim.18.gain_ref
  1.3 0.7 iota_compare_fusion
  2.0 2.5 %select_reduce_fusion.subject_ref = bf16[64,640]{1,0:T(8,128)(2,1)} fusion(bf16[64,16,640]{2,1,0:T(8,128)(2,1)} %param.6, pred[64,16]{1,0:T(8,128)(4,1)S(1)} %iota_compare_fusion), kind=kLoop, calls=%fused_computation | loop fusion | flops 1269760 | bytes 1393664 | tf_op jit(solution)/shard_map/reduce_sum | solution.py:740
  4.5 62.9 %make_keys.1.keys_ref = bf16[128,1024]{1,0:T(8,128)(2,1)} custom-call(bf16[64,640]{1,0:T(8,128)(2,1)} %select_reduce_fusion.subject_ref, f32[1,640]{1,0:T(1,128)} %broadcast_in_dim.18.gain_ref, bf16[640,1024]{1,0:T(8,128)(2,1)} %gate_ref.1, bf16[640,1024]{1,0:T(8,128)(2,1)} %up_ref.1), custom_call_target="tpu_custom_call" | custom-call | tf_op jit(solution)/shard_map/make_keys/pallas_call | solution.py:401
  67.4 4.0 %convert.5 = bf16[1024,2048]{1,0:T(8,128)(2,1)S(1)} convert(f32[1024,2048]{1,0:T(8,128)} %cov_ref.1) | non-fusion elementwise | flops 2097152 | bytes 12582912 | tf_op jit(solution)/shard_map/convert.2
  71.4 0.7 slice.11.covc_ref
  72.2 0.1 slice_bitcast_fusion
  72.2 0.8 copy.7.covr_ref
  73.0 117.7 %spread_keys.1 = (bf16[16,128,1024]{2,1,0:T(8,128)(2,1)}, bf16[16,64,1024]{2,1,0:T(8,128)(2,1)}, bf16[8,64,1024]{2,1,0:T(8,128)(2,1)}, bf16[8,64,1024]{2,1,0:T(8...) custom-call(bf16[128,1024]{1,0:T(8,128)(2,1)} %make_keys.1.keys_ref, ...), custom_call_target="tpu_custom_call" | custom-call | tf_op jit(solution)/shard_map/spread_keys/pallas_call | solution.py:562
  190.7 29.8 %factor_corner.1.inv_ref = f32[512,512]{1,0:T(8,128)} custom-call(bf16[8,64,1024]{2,1,0:T(8,128)(2,1)} %get-tuple-element.13.k5_ref, bf16[8,64,512]{2,1,0:T(8,128)(2,1)} %get-tuple-element.16.jj_ref), custom_call_target="tpu_custom_call" | custom-call | tf_op jit(solution)/shard_map/factor_corner/pallas_call | solution.py:653
  220.5 20.6 %update_lower.1 = f32[1024,2048]{1,0:T(8,128)} custom-call(f32[1024,2048]{1,0:T(8,128)} %cov_ref.1, bf16[16,128,1024]{2,1,0:T(8,128)(2,1)} %get-tuple-element.11.kc_ref, bf16[16,64,1024]{2,1,0:T(8,128)(2,1)} %get-tuple-element.12.kr_ref, bf16[8,64,1024]{2,1,0:T(8,128)(2,1)} %get-tuple-element.13.k5_ref, bf16[8,64,1024]{2,1,0:T(8,128)(2,1)} %get-tuple-element.14.cr_ref, ...), custom_call_target="tpu_custom_call" | custom-call | tf_op jit(solution)/shard_map/update_lower/pallas_call | solution.py:723

commit v2 on v1

v2 whole, which is shorter than its diff:
```python
import functools

import jax
import jax.numpy as jnp
from jax import lax
from jax.experimental import pallas as pl
from jax.experimental.pallas import tpu as pltpu
from jax.sharding import Mesh
from jax.sharding import PartitionSpec as P

MESH = pl.DeviceIdType.MESH
BF16 = jnp.bfloat16
F32 = jnp.float32
EPSILON = 1e-06
HIDDEN = 16384
WIDTH = 5120
PROMPTS = 1024
VMEM_LIMIT = 60 * 1024 * 1024
BASE = 16


def here():
    return tuple(lax.axis_index(name) for name in ("x", "y", "z", "k"))


def moved(position, axis, step):
    place = list(position)
    size = 2 if axis == 3 else 4
    place[axis] = lax.rem(place[axis] + (step % size), size)
    return tuple(place)


def remote(src, dst, send, recv, target):
    return pltpu.make_async_remote_copy(
        src_ref=src, dst_ref=dst, send_sem=send, recv_sem=recv, device_id=target, device_id_type=MESH
    )


def greet(targets):
    barrier = pltpu.get_barrier_semaphore()
    for target in targets:
        pl.semaphore_signal(barrier, inc=1, device_id=target, device_id_type=MESH)
    pl.semaphore_wait(barrier, len(targets))


def when(condition, action):
    if condition is None:
        action()
    else:
        pl.when(condition)(action)


class PlaneGather:
    SENT = (
        (0, 0, 1, 1, None), (0, 0, 1, -1, None), (-1, 0, 1, 1, 0), (1, 0, 1, -1, 1),
        (0, 0, 0, 1, None), (-1, 0, 0, 1, None), (1, 0, 0, 1, None), (2, 0, 0, 1, None),
        (0, 0, 0, -1, None), (-1, 0, 0, -1, None), (1, 0, 0, -1, None), (2, 0, 0, -1, None),
        (0, -1, 0, 1, None), (-1, -1, 0, 1, None), (1, 1, 0, -1, None), (2, 1, 0, -1, None),
    )
    GOT = (
        (-1, 0, None), (1, 0, None), (2, 0, 0), (2, 0, 1),
        (0, -1, None), (-1, -1, None), (1, -1, None), (2, -1, None),
        (0, 1, None), (-1, 1, None), (1, 1, None), (2, 1, None),
        (0, 2, None), (-1, 2, None), (1, 2, None), (2, 2, None),
    )
    EVENTS = (
        ((0,), (2, 5, 9)), ((1,), (3, 6, 10)), ((4,), (12,)), ((8,), ()), ((2, 3), (7, 11)), ((5,), (13,)), ((10,), (14,)),
        ((9,), ()), ((6,), ()), ((11,), (15,)), ((7,), ()), ((12,), ()), ((13,), ()), ((14,), ()), ((15,), ()),
    )
    PLACES = tuple(((-1, 0), (1, 0), (0, -1), (0, 1), (2, 0), (-1, -1), (1, 1), (-1, 1), (1, -1), (2, 1), (2, -1), (0, 2), (-1, 2), (1, 2), (2, 2)))

    def __init__(self, buf, rows, send, recv, pos, only=None):
        self.buf, self.rows, self.send, self.recv, self.pos, self.only = buf, rows, send, recv, pos, only

    def block(self, half, first, second):
        dx, dy = (second, first) if half == 0 else (first, second)
        return lax.rem(self.pos[0] + dx % 4, 4), lax.rem(self.pos[1] + dy % 4, 4)

    def piece(self, half, first, second, part=None):
        size = self.rows // 2
        start = half * size
        if part is not None:
            size //= 2
            start += part * size
        bx, by = self.block(half, first, second)
        return self.buf.at[bx, by, pl.ds(start, size)]

    def cond(self, half, first, second):
        return None if self.only is None else self.only(*self.block(half, first, second))

    def copy(self, half, kind, first, second, axis, step, part=None):
        axis = axis if half == 0 else 1 - axis
        ref = self.piece(half, first, second, part)
        return remote(ref, ref, self.send.at[half, kind], self.recv.at[half, kind], moved(self.pos, axis, step))

    def go(self, half, kind):
        first, second, axis, step, part = self.SENT[kind]
        when(self.cond(half, first, second), lambda: self.copy(half, kind, first, second, axis, step, part).start())

    def arrive(self, half, kind):
        first, second, part = self.GOT[kind]
        when(self.cond(half, first, second), lambda: self.copy(half, kind, first, second, 0, 1, part).wait_recv())

    def begin(self):
        for kind in (0, 1, 4, 8):
            for half in (0, 1):
                self.go(half, kind)

    def event(self, number, half):
        kinds, on = self.EVENTS[number]
        for kind in kinds:
            self.arrive(half, kind)
        for kind in on:
            self.go(half, kind)

    def finish(self):
        for half in (0, 1):
            for kind in range(16):
                first, second, axis, step, part = self.SENT[kind]
                when(
                    self.cond(half, first, second),
                    lambda: self.copy(half, kind, first, second, axis, step, part).wait_send(),
                )


class ColumnGather:
    def __init__(self, buf, send, recv, pos):
        self.buf, self.send, self.recv, self.pos = buf, send, recv, pos

    def piece(self, dz, dk=0, part=None):
        z, k = self.pos[2], self.pos[3]
        slot = lax.rem(z + dz % 4, 4) * 2 + lax.rem(k + dk, 2)
        if part is None:
            return self.buf.at[slot]
        return self.buf.at[slot, pl.ds(32 * part, 32)]

    SENT = {0: (0, 2, 1, None), 1: (0, 2, -1, None), 2: (-1, 2, 1, 0), 3: (1, 2, -1, 1),
            4: (0, 3, 1, None), 5: (-1, 3, 1, None), 6: (1, 3, 1, None), 7: (2, 3, 1, None)}
    GOT = {0: (-1, 0, None), 1: (1, 0, None), 2: (2, 0, 0), 3: (2, 0, 1),
           4: (0, 1, None), 5: (-1, 1, None), 6: (1, 1, None), 7: (2, 1, None)}

    def go(self, kind):
        dz, axis, step, part = self.SENT[kind]
        ref = self.piece(dz, 0, part)
        remote(ref, ref, self.send.at[kind], self.recv.at[kind], moved(self.pos, axis, step)).start()

    def arrive(self, kind):
        dz, dk, part = self.GOT[kind]
        ref = self.piece(dz, dk, part)
        remote(ref, ref, self.send.at[kind], self.recv.at[kind], moved(self.pos, 2, 1)).wait_recv()

    def begin(self):
        for kind in (0, 1, 4):
            self.go(kind)

    def middle(self):
        self.arrive(0)
        self.go(2)
        self.go(5)
        self.arrive(1)
        self.go(3)
        self.go(6)

    def end(self):
        self.arrive(2)
        self.arrive(3)
        self.go(7)
        for kind in (4, 5, 6, 7):
            self.arrive(kind)

    def finish(self):
        for kind in range(8):
            dz, axis, step, part = self.SENT[kind]
            ref = self.piece(dz, 0, part)
            remote(ref, ref, self.send.at[kind], self.recv.at[kind], moved(self.pos, axis, step)).wait_send()


def column_peers(pos):
    peers = []
    for dz in range(4):
        for dk in range(2):
            if dz or dk:
                peers.append(moved(moved(pos, 2, dz), 3, dk))
    return peers


def to_all_columns(buf, send, recv, pos):
    copies = []
    mine = pos[2] * 2 + pos[3]
    number = 0
    for dz in range(4):
        for dk in range(2):
            if dz == 0 and dk == 0:
                continue
            target = moved(moved(pos, 2, dz), 3, dk)
            out = remote(buf.at[mine], buf.at[mine], send.at[number], recv.at[number], target)
            origin = moved(moved(pos, 2, -dz), 3, -dk)
            slot = origin[2] * 2 + origin[3]
            into = remote(buf.at[slot], buf.at[slot], send.at[number], recv.at[number], target)
            copies.append((out, into))
            number += 1
    return copies


def to_axis(buf, send, recv, pos, axis):
    copies = []
    mine = pos[axis]
    for step in (1, 2, 3):
        target = moved(pos, axis, step)
        out = remote(buf.at[mine], buf.at[mine], send.at[step - 1], recv.at[step - 1], target)
        slot = moved(pos, axis, -step)[axis]
        into = remote(buf.at[slot], buf.at[slot], send.at[step - 1], recv.at[step - 1], target)
        copies.append((out, into))
    return copies


def exchange(copies):
    for out, _ in copies:
        out.start()
    for _, into in copies:
        into.wait_recv()


def keys_kernel(
    subject_ref, gain_ref, gate_ref, up_ref, cov_ref, keys_ref, cc, jj_ref, cr_ref,
    xx, own_w, other_w, sel_w, squares, part, hop_out, hop_in, total, sum_y, sum_x, sum_c, cov_rows, cov_cols,
    local_sem, w_send, w_recv, sq_send, sq_recv, x_send, x_recv, sib_send, sib_recv,
    hop_send, hop_recv, sy_send, sy_recv, sx_send, sx_recv, sc_send, sc_recv, cc_send, cc_recv,
):
    pos = here()
    x, y, z, k = pos
    sibling = moved(pos, 3, 1)
    col = z * 2 + k
    plane = [moved(pos, axis, step) for axis in (0, 1) for step in (1, 2, 3)]
    greet(plane + column_peers(pos))

    weights = ((gate_ref, 0), (up_ref, 1))

    def swap(ref, index):
        return remote(ref, other_w.at[index], w_send.at[index], w_recv.at[index], sibling)

    def fetch(ref, index):
        return pltpu.make_async_copy(ref, own_w.at[index], local_sem.at[index])

    fetch_rows = pltpu.make_async_copy(cov_ref.at[pl.ds(0, 64)], cov_rows, local_sem.at[2])
    fetch_cols = pltpu.make_async_copy(cov_ref.at[:, pl.ds(0, 128)], cov_cols, local_sem.at[3])

    subject = subject_ref[...].astype(F32)
    squared = subject * subject
    folded = squared[:, 0:128]
    for group in range(1, 5):
        folded = folded + squared[:, group * 128 : (group + 1) * 128]
    squares[col] = folded
    square_copies = to_all_columns(squares, sq_send, sq_recv, pos)
    for out, _ in square_copies:
        out.start()
    for ref, index in weights:
        fetch(ref, index).start()
        swap(ref, index).start()
    fetch_rows.start()
    fetch_cols.start()

    def select(source, core):
        def body(step, carry):
            for index in range(2):
                low = source[index, :, pl.ds(pl.multiple_of(step * 128, 128), 128)]
                high = source[index, :, pl.ds(pl.multiple_of(512 + step * 128, 128), 128)]

                @pl.when(k == 0)
                def _():
                    sel_w[step, pl.ds(pl.multiple_of(core * 640, 128), 640), pl.ds(index * 128, 128)] = jnp.concatenate(
                        [low[:, :64], high[:, :64]], axis=1
                    )

                @pl.when(k == 1)
                def _():
                    sel_w[step, pl.ds(pl.multiple_of(core * 640, 128), 640), pl.ds(index * 128, 128)] = jnp.concatenate(
                        [low[:, 64:], high[:, 64:]], axis=1
                    )

            return carry

        lax.fori_loop(0, 4, body, 0)

    for _, into in square_copies:
        into.wait_recv()
    everyone = squares[0]
    for member in range(1, 8):
        everyone = everyone + squares[member]
    inverse_rms = lax.rsqrt(jnp.sum(everyone, axis=1, keepdims=True) / WIDTH + EPSILON)
    xx[k, x, y] = (subject * inverse_rms * gain_ref[...]).astype(BF16)

    gather = PlaneGather(xx.at[k], 64, x_send, x_recv, pos)
    gather.begin()

    def to_sibling(half, number, first, second):
        ref = gather.piece(half, first, second)
        return remote(ref, ref, sib_send.at[half, number], sib_recv.at[half, number], sibling)

    def from_sibling(half, number, first, second):
        bx, by = gather.block(half, first, second)
        ref = xx.at[1 - k, bx, by, pl.ds(half * 32, 32)]
        return remote(ref, ref, sib_send.at[half, number], sib_recv.at[half, number], sibling)

    places = ((0, 0),) + PlaneGather.PLACES
    for half in (0, 1):
        to_sibling(half, 0, 0, 0).start()

    for ref, index in weights:
        fetch(ref, index).wait()
    select(own_w, k)

    def arrivals(numbers):
        for number in numbers:
            for half in (0, 1):
                gather.event(number, half)
                to_sibling(half, number + 1, *places[number + 1]).start()

    def siblings(numbers):
        for number in numbers:
            for half in (0, 1):
                from_sibling(half, number, *places[number]).wait_recv()

    def line(core, half, second):
        if half == 0:
            value = xx[core, lax.rem(x + second % 4, 4), :, 0:32, :]
        else:
            value = xx[core, :, lax.rem(y + second % 4, 4), 32:64, :]
        return value.reshape(128, 640)

    def product(chunk, dest):
        second = (0, -1, 1, 2)[chunk]
        value = None
        for core in (0, 1):
            left = jnp.concatenate([line(core, 0, second), line(core, 1, second)], axis=0)
            term = jnp.dot(left, sel_w[dest, core * 640 : core * 640 + 640], preferred_element_type=F32)
            value = term if value is None else value + term
        return value

    def dest(step):
        return lax.rem(z + step % 4, 4)

    def hop(chunk, kind):
        target = moved(pos, 2, 1 if kind % 2 == 0 else -1)
        return remote(
            hop_out.at[chunk, kind], hop_in.at[chunk, kind], hop_send.at[chunk, kind], hop_recv.at[chunk, kind], target
        )

    def send(chunk, kind, value):
        hop_out[chunk, kind] = value.astype(BF16)
        hop(chunk, kind).start()

    def multiply(chunk):
        value = product(chunk, dest(2))
        send(chunk, 0, value[:128])
        send(chunk, 1, value[128:])
        value = product(chunk, dest(1))
        send(chunk, 2, value[128:])
        part[chunk, 0] = value[:128]
        value = product(chunk, dest(-1))
        send(chunk, 3, value[:128])
        part[chunk, 1] = value[128:]
        value = product(chunk, dest(0))
        part[chunk, 2] = value[:128]
        part[chunk, 3] = value[128:]

    def join(chunk):
        hop(chunk, 0).wait_recv()
        send(chunk, 4, part[chunk, 0] + hop_in[chunk, 0].astype(F32))
        hop(chunk, 1).wait_recv()
        send(chunk, 5, part[chunk, 1] + hop_in[chunk, 1].astype(F32))

    def finish(chunk):
        second = (0, -1, 1, 2)[chunk]
        for half in (0, 1):
            kinds = (4, 3) if half == 0 else (2, 5)
            for kind in kinds:
                hop(chunk, kind).wait_recv()
            value = part[chunk, 2 + half] + (hop_in[chunk, kinds[0]].astype(F32) + hop_in[chunk, kinds[1]].astype(F32))
            gate, up = value[:, :128], value[:, 128:]
            raw = gate / (1.0 + jnp.exp(-gate)) * up
            place = lax.rem((x if half == 0 else y) + second % 4, 4)
            total[:, pl.ds(pl.multiple_of(half * 512 + place * 128, 128), 128)] = raw.T

    covs = PlaneGather(cc, 64, cc_send, cc_recv, pos, only=lambda bx, by: bx < 2)

    def cov_events(numbers):
        for number in numbers:
            for half in (0, 1):
                covs.event(number, half)

    arrivals((0, 1, 4))
    for ref, index in weights:
        swap(ref, index).wait_recv()
    select(other_w, 1 - k)
    arrivals((2, 3))
    siblings((0, 1, 2, 5))
    multiply(0)
    arrivals((5, 8, 10))
    siblings((3, 6, 9, 11))
    multiply(1)
    join(0)
    arrivals((6, 7, 9))
    siblings((4, 7, 8, 10))
    multiply(2)
    join(1)
    arrivals((11, 12, 13, 14))

    fetch_rows.wait()

    @pl.when(x < 2)
    def _():
        cc[x, y] = cov_rows[...].astype(BF16)

    covs.begin()
    siblings((12, 13, 14, 15))
    multiply(3)
    join(2)
    fetch_cols.wait()
    cr_ref[...] = cov_cols[...].T[0:64].astype(BF16)
    cov_events((0, 1))
    finish(0)
    cov_events((2, 3, 4))
    join(3)
    finish(1)
    cov_events((5, 6))
    finish(2)
    cov_events((7, 8, 9))
    finish(3)
    raw = total[...]
    mass = jnp.sum(raw * raw, axis=0, keepdims=True)
    sum_y[y] = jnp.broadcast_to(mass, (8, PROMPTS))
    y_copies = to_axis(sum_y, sy_send, sy_recv, pos, 1)
    exchange(y_copies)
    sum_x[x] = sum_y[0] + sum_y[1] + sum_y[2] + sum_y[3]
    x_copies = to_axis(sum_x, sx_send, sx_recv, pos, 0)
    exchange(x_copies)
    sum_c[col] = sum_x[0] + sum_x[1] + sum_x[2] + sum_x[3]
    c_copies = to_all_columns(sum_c, sc_send, sc_recv, pos)
    exchange(c_copies)
    mass = sum_c[0]
    for member in range(1, 8):
        mass = mass + sum_c[member]
    scale = lax.rsqrt(mass[0:1] / HIDDEN + EPSILON)
    keys_ref[...] = (raw * scale).astype(BF16)
    cov_events((10, 11, 12, 13, 14))
    jj_ref[...] = cc[:, :, :, 0:128].reshape(512, 128).astype(F32).T[0:64].astype(BF16)

    for ref, index in weights:
        swap(ref, index).wait_send()
    for copies in (square_copies, y_copies, x_copies, c_copies):
        for out, _ in copies:
            out.wait_send()
    gather.finish()
    covs.finish()
    for half in (0, 1):
        for number in range(16):
            to_sibling(half, number, *places[number]).wait_send()
    for chunk in range(4):
        for kind in range(6):
            hop(chunk, kind).wait_send()


def make_keys(subject, gain, w_gate, w_up, cov):
    dma = pltpu.SemaphoreType.DMA
    vmem = pl.BlockSpec(memory_space=pltpu.VMEM)
    return pl.pallas_call(
        keys_kernel,
        name="make_keys",
        out_shape=(
            jax.ShapeDtypeStruct((128, PROMPTS), BF16),
            jax.ShapeDtypeStruct((2, 4, 64, 2048), BF16),
            jax.ShapeDtypeStruct((64, 512), BF16),
            jax.ShapeDtypeStruct((64, 1024), BF16),
        ),
        in_specs=[vmem] * 2 + [pl.BlockSpec(memory_space=pl.ANY)] * 3,
        out_specs=(vmem,) * 4,
        scratch_shapes=[
            pltpu.VMEM((2, 4, 4, 64, 640), BF16),
            pltpu.VMEM((2, 640, 1024), BF16),
            pltpu.VMEM((2, 640, 1024), BF16),
            pltpu.VMEM((4, 1280, 256), BF16),
            pltpu.VMEM((8, 64, 128), F32),
            pltpu.VMEM((4, 4, 128, 256), F32),
            pltpu.VMEM((4, 6, 128, 256), BF16),
            pltpu.VMEM((4, 6, 128, 256), BF16),
            pltpu.VMEM((128, PROMPTS), F32),
            pltpu.VMEM((4, 8, PROMPTS), F32),
            pltpu.VMEM((4, 8, PROMPTS), F32),
            pltpu.VMEM((8, 8, PROMPTS), F32),
            pltpu.VMEM((64, 2048), F32),
            pltpu.VMEM((1024, 128), F32),
            dma((4,)), dma((2,)), dma((2,)), dma((7,)), dma((7,)), dma((2, 16)), dma((2, 16)), dma((2, 16)), dma((2, 16)),
            dma((4, 6)), dma((4, 6)), dma((3,)), dma((3,)), dma((3,)), dma((3,)), dma((7,)), dma((7,)), dma((2, 16)), dma((2, 16)),
        ],
        compiler_params=pltpu.CompilerParams(collective_id=0, has_side_effects=True, vmem_limit_bytes=VMEM_LIMIT),
    )(subject, gain, w_gate, w_up, cov)


def split(value):
    high = value.astype(BF16)
    return high, (value - high.astype(F32)).astype(BF16)


def dot3(left, right, dims):
    lh, ll = split(left)
    rh, rl = split(right)
    dot = functools.partial(lax.dot_general, dimension_numbers=(dims, ((), ())), preferred_element_type=F32)
    return dot(lh, rh) + (dot(lh, rl) + dot(ll, rh))


def small_factor(work, extra):
    lane = lax.broadcasted_iota(jnp.int32, (1, 128), 1)

    def body(step, carry):
        start = pl.multiple_of(step * BASE, BASE)
        rows = work[pl.ds(start, BASE), :]
        turned = pltpu.roll(rows[:, :128], lax.rem(128 - start, 128), 1)
        entry = [[jnp.broadcast_to(turned[i : i + 1, j : j + 1], (1, 128)) for j in range(i + 1)] for i in range(BASE)]
        solved = []
        for j in range(BASE):
            inverse = lax.rsqrt(entry[j][j])
            row = rows[j : j + 1, :]
            for m in range(j):
                row = row - jnp.concatenate([entry[j][m]] * 2, axis=1) * solved[m]
            solved.append(row * jnp.concatenate([inverse] * 2, axis=1))
            for i in range(j + 1, BASE):
                entry[i][j] = entry[i][j] * inverse
            for i in range(j + 1, BASE):
                for m in range(j + 1, i + 1):
                    entry[i][m] = entry[i][m] - entry[i][j] * entry[m][j]
        block = jnp.concatenate(solved, axis=0)
        work[pl.ds(start, BASE), :] = block
        later = jnp.where(lane >= start + BASE, block[:, :128], 0.0)
        lh, ll = split(later)
        rh, rl = split(block)
        left = jnp.concatenate([lh, lh, ll], axis=0)
        right = jnp.concatenate([rh, rl, rh], axis=0)
        work[...] = work[...] - lax.dot_general(left, right, (((0,), (0,)), ((), ())), preferred_element_type=F32)
        for number, action in extra.items():
            pl.when(step == number)(action)
        return carry

    lax.fori_loop(0, 128 // BASE, body, 0)


def factor(aug, work, extras):
    eye = (lax.broadcasted_iota(jnp.int32, (128, 128), 0) == lax.broadcasted_iota(jnp.int32, (128, 128), 1)).astype(F32)
    for number in range(4):
        lo, hi = number * 128, (number + 1) * 128
        work[:, 0:128] = aug[lo:hi, lo:hi]
        work[:, 128:256] = eye
        small_factor(work, extras[number])
        inverse = work[:, 128:256]
        if hi < 512:
            right = dot3(inverse, aug[lo:hi, hi : 512 + lo], ((1,), (0,)))
            full = jnp.concatenate([right, inverse], axis=1)
            aug[lo:hi, hi : 512 + hi] = full
            ahead = right[:, 0 : 512 - hi]
            aug[hi:512, hi : 512 + hi] = aug[hi:512, hi : 512 + hi] - dot3(ahead, full, ((0,), (0,)))
        else:
            aug[lo:hi, 512 : 512 + lo] = dot3(inverse, aug[lo:hi, 512 : 512 + lo], ((1,), (0,)))
            aug[lo:hi, 512 + lo : 512 + hi] = inverse


def spread_kernel(
    keys_ref, jjb_ref, crb_ref, kc, kr, k5, cr, inv_ref, first, jj, aug, work,
    kc_send, kc_recv, k5_send, k5_recv, cr_send, cr_recv, jj_send, jj_recv, f_send, f_recv, row_send, row_recv, local_sem,
):
    pos = here()
    x, y, z, k = pos
    sibling = moved(pos, 3, 1)
    row = x * 4 + y
    col = z * 2 + k
    plane = [moved(pos, axis, step) for axis in (0, 1) for step in (1, -1)]
    ring = [moved(pos, 2, 1), moved(pos, 2, -1), sibling]
    greet(plane + ring)

    @pl.when(row == 0)
    def _():
        first[0, 0] = keys_ref[0:64]

    first_tile = PlaneGather(first, 64, f_send, f_recv, pos, only=lambda bx, by: (bx == 0) & (by == 0))
    first_tile.begin()
    jj[col] = jjb_ref[...]
    corner = ColumnGather(jj, jj_send, jj_recv, pos)
    corner.begin()
    kc[x, y] = keys_ref[...]
    keys = PlaneGather(kc, 128, kc_send, kc_recv, pos)
    keys.begin()

    source = lax.rem(row, 8)
    source_z = source // 2
    upper = row // 8
    away = lax.rem(z + 4 - source_z, 4)
    same = k == lax.rem(source, 2)
    places = ((0, 0),) + PlaneGather.PLACES

    def wave(number, kind, own=False):
        one, two = keys.block(0, *places[number]), keys.block(1, *places[number])
        bx = jnp.where(upper == 0, one[0], two[0])
        by = jnp.where(upper == 0, one[1], two[1])
        part = kind % 2
        dst = kr.at[bx, by, pl.ds(part * 32, 32)]
        src = kc.at[bx, by, pl.ds(pl.multiple_of(upper * 64 + part * 32, 32), 32)] if own else dst
        target = sibling if kind >= 2 else moved(pos, 2, 1 if kind == 0 else -1)
        return remote(src, dst, row_send.at[number, kind], row_recv.at[number, kind], target)

    def own_copy(number):
        one, two = keys.block(0, *places[number]), keys.block(1, *places[number])
        bx = jnp.where(upper == 0, one[0], two[0])
        by = jnp.where(upper == 0, one[1], two[1])
        return pltpu.make_async_copy(
            kc.at[bx, by, pl.ds(pl.multiple_of(upper * 64, 64), 64)], kr.at[bx, by], local_sem.at[number]
        )

    def relay(number):
        if number < 16:

            @pl.when(same & (away == 0))
            def _():
                for kind in (0, 1, 2, 3):
                    wave(number, kind, own=True).start()
                own_copy(number).start()

        for distance in (1, 2, 3):
            for kind, lag in ((0, distance), (1, 4 - distance)):
                block = number - lag
                if 0 <= block < 16:

                    @pl.when(same & (away == distance))
                    def _():
                        wave(block, kind).wait_recv()
                        if lag < 3:
                            wave(block, kind).start()
                        wave(block, kind + 2).start()

    def key_event(number):
        if number < 15:
            keys.event(number, 0)
            keys.event(number, 1)
        relay(number + 1)

    cr[col] = crb_ref[...]
    panel_rows = ColumnGather(cr, cr_send, cr_recv, pos)

    for number in range(15):
        first_tile.event(number, 0)
        first_tile.event(number, 1)
    k5[col] = first[0, 0]
    first_keys = ColumnGather(k5, k5_send, k5_recv, pos)
    first_keys.begin()
    corner.middle()
    relay(0)
    key_event(0)
    first_keys.middle()
    corner.end()
    key_event(1)
    first_keys.end()
    panel_rows.begin()
    key_event(2)

    corner_keys = k5[...].reshape(512, PROMPTS)
    outer = lax.dot_general(corner_keys, corner_keys, (((1,), (1,)), ((), ())), preferred_element_type=F32)
    aug[:, 0:512] = jj[...].reshape(512, 512).astype(F32) + outer * (1.0 / PROMPTS)
    aug[:, 512:1024] = (
        lax.broadcasted_iota(jnp.int32, (512, 512), 0) == lax.broadcasted_iota(jnp.int32, (512, 512), 1)
    ).astype(F32)
    beside = [functools.partial(key_event, number) for number in range(3, 18)]
    beside.insert(2, panel_rows.middle)
    beside.insert(5, panel_rows.end)
    extras = [{} for _ in range(4)]
    for number, action in enumerate(beside):
        extras[number // 8][number % 8] = action
    factor(aug, work, extras)
    inv_ref[...] = aug[:, 512:1024]

    for number in range(16):

        @pl.when(k != lax.rem(source, 2))
        def _():
            wave(number, 2).wait_recv()
            wave(number, 3).wait_recv()

        @pl.when(same & (away == 0))
        def _():
            for kind in range(4):
                wave(number, kind, own=True).wait_send()
            own_copy(number).wait()

        for distance in (1, 2, 3):

            @pl.when(same & (away == distance))
            def _():
                for kind, lag in ((0, distance), (1, 4 - distance)):
                    if lag < 3:
                        wave(number, kind).wait_send()
                    wave(number, kind + 2).wait_send()

    first_tile.finish()
    keys.finish()
    panel_rows.finish()
    first_keys.finish()
    corner.finish()


def spread(keys, jjb, crb):
    dma = pltpu.SemaphoreType.DMA
    vmem = pl.BlockSpec(memory_space=pltpu.VMEM)
    return pl.pallas_call(
        spread_kernel,
        name="spread_factor",
        out_shape=(
            jax.ShapeDtypeStruct((4, 4, 128, PROMPTS), BF16),
            jax.ShapeDtypeStruct((4, 4, 64, PROMPTS), BF16),
            jax.ShapeDtypeStruct((8, 64, PROMPTS), BF16),
            jax.ShapeDtypeStruct((8, 64, 1024), BF16),
            jax.ShapeDtypeStruct((512, 512), F32),
        ),
        in_specs=[vmem] * 3,
        out_specs=(vmem,) * 5,
        scratch_shapes=[
            pltpu.VMEM((1, 1, 64, PROMPTS), BF16),
            pltpu.VMEM((8, 64, 512), BF16),
            pltpu.VMEM((512, 1024), F32),
            pltpu.VMEM((128, 256), F32),
            dma((2, 16)), dma((2, 16)), dma((8,)), dma((8,)), dma((8,)), dma((8,)), dma((8,)), dma((8,)), dma((2, 16)), dma((2, 16)),
            dma((16, 4)), dma((16, 4)), dma((16,)),
        ],
        compiler_params=pltpu.CompilerParams(collective_id=1, has_side_effects=True, vmem_limit_bytes=VMEM_LIMIT),
    )(keys, jjb, crb)


def update_kernel(cov_ref, kc_ref, kr_ref, k5_ref, cr_ref, cc_ref, inv_ref, out_ref, covb, outb, panel, in_sem, out_sem):
    x, y, z, k = here()
    row = x * 4 + y
    col = z * 2 + k
    scale = 1.0 / PROMPTS
    nt = (((1,), (1,)), ((), ()))
    nn = (((1,), (0,)), ((), ()))
    tn = (((0,), (0,)), ((), ()))
    dot = functools.partial(lax.dot_general, preferred_element_type=F32)

    def load(step):
        area = (pl.ds(step * 128, 1024 - step * 128), pl.ds(step * 256, 256))
        return pltpu.make_async_copy(cov_ref.at[area], covb.at[step % 2, pl.ds(step * 128, 1024 - step * 128)], in_sem.at[step % 2])

    def store(step):
        return pltpu.make_async_copy(outb.at[step % 2], out_ref.at[:, pl.ds(step * 256, 256)], out_sem.at[step % 2])

    load(0).start()
    load(1).start()
    inverse = inv_ref[...]
    inverse_high = inverse.astype(BF16)
    first = k5_ref[...].reshape(512, PROMPTS)
    rows = kr_ref[...].reshape(1024, PROMPTS)
    matrix_rows = cr_ref[...].reshape(512, 1024).astype(F32) + dot(first, rows, nt) * scale
    high, low = split(matrix_rows)
    panel[...] = dot(inverse_high, high, nn)
    own = inv_ref[pl.ds(pl.multiple_of(col * 64, 64), 64), :]
    own_high, own_low = split(own)
    own_panel = dot(own_high, high, nn) + (dot(own_low, high, nn) + dot(own_high, low, nn))
    panel_low = panel[...].astype(BF16)
    for step in range(8):
        top = step * 128
        height = 1024 - top
        load(step).wait()
        if step >= 2:
            store(step - 2).wait()
        cols = kc_ref[2 * step : 2 * step + 2].reshape(256, PROMPTS)
        matrix_cols = cc_ref[:, :, step * 256 : (step + 1) * 256].reshape(512, 256).astype(F32) + dot(first, cols, nt) * scale
        panel_cols = dot(inverse_high, matrix_cols.astype(BF16), nn).astype(BF16)
        value = covb[step % 2, top:1024] + dot(rows[top:], cols, nt) * scale - dot(panel_low[:, top:], panel_cols, tn)
        if step == 0:
            value = jnp.concatenate([own_panel.T, value[:, 64:]], axis=1)
        i = lax.broadcasted_iota(jnp.int32, (height, 256), 0) + top
        j = lax.broadcasted_iota(jnp.int32, (height, 256), 1) + step * 256
        row_global = (i // 64 * 16 + row) * 64 + i % 64
        col_global = (j // 64 * 8 + col) * 64 + j % 64
        outb[step % 2, top:1024] = jnp.where(row_global >= col_global, value, 0.0)
        if step:
            outb[step % 2, 0:top] = jnp.zeros((top, 256), F32)
        store(step).start()
        if step + 2 < 8:
            load(step + 2).start()
    store(6).wait()
    store(7).wait()


def update(cov, kc, kr, k5, cr, cc, inverse):
    dma = pltpu.SemaphoreType.DMA
    vmem = pl.BlockSpec(memory_space=pltpu.VMEM)
    return pl.pallas_call(
        update_kernel,
        name="update_lower",
        out_shape=jax.ShapeDtypeStruct((1024, 2048), F32),
        in_specs=[pl.BlockSpec(memory_space=pl.ANY)] + [vmem] * 6,
        out_specs=pl.BlockSpec(memory_space=pl.ANY),
        scratch_shapes=[
            pltpu.VMEM((2, 1024, 256), F32), pltpu.VMEM((2, 1024, 256), F32), pltpu.VMEM((512, 1024), F32), dma((2,)), dma((2,)),
        ],
        compiler_params=pltpu.CompilerParams(vmem_limit_bytes=VMEM_LIMIT),
    )(cov, kc, kr, k5, cr, cc, inverse)


def on_device(residual, positions, norm_gain, w_gate, w_up, covariance):
    prompts, tokens, _ = residual.shape
    token = lax.broadcasted_iota(jnp.int32, (prompts, tokens), 1)
    picked = jnp.where((token == positions[:, None])[:, :, None], residual, jnp.zeros_like(residual))
    subject = jnp.sum(picked.astype(F32), axis=1).astype(BF16)
    keys, cc, jjb, crb = make_keys(subject, norm_gain[None, :], w_gate, w_up, covariance)
    kc, kr, k5, cr, inverse = spread(keys, jjb, crb)
    kc = kc.reshape(16, 128, PROMPTS)
    kr = kr.reshape(16, 64, PROMPTS)
    cc = cc.reshape(8, 64, 2048)
    return update(covariance, kc, kr, k5, cr, cc, inverse)


def solution(mesh):
    torus = Mesh(mesh.devices.reshape(4, 4, 4, 2), ("x", "y", "z", "k"))
    row, col = ("x", "y"), ("z", "k")
    placed = (P(row, None, col), P(row), P(col), P(col, row), P(col, row), P(row, col))
    return jax.shard_map(on_device, mesh=torus, in_specs=placed, out_specs=P(row, col), check_vma=False)
```

time: 242 us -> 191 us (0.79)
  the two profiles are of different devices: /device:TPU:69 before, /device:TPU:20 now
where the time goes in v2:
time: 191 us
  Pallas kernels  186 us (97%)
  other arithmetic  3.25 us (2%)
    pallas_call x1, Pallas kernels, spread(): pl.pallas_call(spread_kernel, name='spread_factor', out_shape=(jax.ShapeD...  96.8 us
    pallas_call x1, Pallas kernels, make_keys(): pl.pallas_call(keys_kernel, name='make_keys', out_shape=(jax.ShapeDtypeSt...  68.6 us
    pallas_call x1, Pallas kernels, update(): pl.pallas_call(update_kernel, name='update_lower', out_shape=jax.ShapeDty...  20.7 us

profile of v2, /device:TPU:20, one launch (start us, length us, event | category | flops | bytes accessed | tf_op | source)
XLA Modules:
  0.0 190.8 jit_solution(7108500537711968666)
XLA Ops:
  0.0 1.3 broadcast_in_dim.18.gain_ref
  1.3 0.7 iota_compare_fusion
  2.0 2.5 %select_reduce_fusion.subject_ref = bf16[64,640]{1,0:T(8,128)(2,1)} fusion(bf16[64,16,640]{2,1,0:T(8,128)(2,1)} %param.6, pred[64,16]{1,0:T(8,128)(4,1)S(1)} %iota_compare_fusion), kind=kLoop, calls=%fused_computation | loop fusion | flops 1269760 | bytes 1393664 | tf_op jit(solution)/shard_map/reduce_sum | solution.py:810
  4.5 68.6 %make_keys.1 = (bf16[128,1024]{1,0:T(8,128)(2,1)}, bf16[2,4,64,2048]{3,2,1,0:T(8,128)(2,1)}, bf16[64,512]{1,0:T(8,128)(2,1)}, bf16[64,1024]{1,0:T(8,128)(2,1)}) custom-call(bf16[64,640]{1,0:T(8,128)(2,1)} %select_reduce_fusion.subject_ref, f32[1,640]{1,0:T(1,128)} %broadcast_in_dim.18.gain_ref, bf16[640,1024]{1,0:T(8,128)(2,1)} %gate_ref.1, ...), custom_call_target="tpu_custom_call" | custom-call | tf_op jit(solution)/shard_map/make_keys/pallas_call | solution.py:467
  73.1 96.8 %spread_factor.1 = (bf16[4,4,128,1024]{3,2,1,0:T(8,128)(2,1)}, bf16[4,4,64,1024]{3,2,1,0:T(8,128)(2,1)}, bf16[8,64,1024]{2,1,0:T(8,128)(2,1)}, bf16[8,64,1024]{2,1,0:T(8,128)(2,1)}, f32[512,512]{1,0:T(8,128)}) custom-call(bf16[128,1024]{1,0:T(8,128)(2,1)} %get-tuple-element.14.keys_ref, bf16[64,512]{1,0:T(8,128)(2,1)} %get-tuple-element.15.jjb_ref, ...), custom_call_target="tpu_custom_call" | custom-call | tf_op jit(solution)/shard_map/spread_factor/pallas_call | solution.py:710
  170.0 20.7 %update_lower.1 = f32[1024,2048]{1,0:T(8,128)} custom-call(f32[1024,2048]{1,0:T(8,128)} %cov_ref.3, bf16[16,128,1024]{2,1,0:T(8,128)(2,1)} %bitcast.3, bf16[16,64,1024]{2,1,0:T(8,128)(2,1)} %bitcast.5, bf16[8,64,1024]{2,1,0:T(8,128)(2,1)} %get-tuple-element.19.k5_ref, bf16[8,64,1024]{2,1,0:T(8,128)(2,1)} %get-tuple-element.20.cr_ref, ...), custom_call_target="tpu_custom_call" | custom-call | tf_op jit(solution)/shard_map/update_lower/pallas_call | solution.py:793

commit v3 on v2

v3 whole, which is shorter than its diff:
```python
import functools

import jax
import jax.numpy as jnp
from jax import lax
from jax.experimental import pallas as pl
from jax.experimental.pallas import tpu as pltpu
from jax.sharding import Mesh
from jax.sharding import PartitionSpec as P

MESH = pl.DeviceIdType.MESH
BF16 = jnp.bfloat16
F32 = jnp.float32
EPSILON = 1e-06
HIDDEN = 16384
WIDTH = 5120
PROMPTS = 1024
VMEM_LIMIT = 60 * 1024 * 1024
BASE = 16
LAG = 2


def here():
    return tuple(lax.axis_index(name) for name in ("x", "y", "z", "k"))


def moved(position, axis, step):
    place = list(position)
    size = 2 if axis == 3 else 4
    place[axis] = lax.rem(place[axis] + (step % size), size)
    return tuple(place)


def remote(src, dst, send, recv, target):
    return pltpu.make_async_remote_copy(
        src_ref=src, dst_ref=dst, send_sem=send, recv_sem=recv, device_id=target, device_id_type=MESH
    )


def greet(targets):
    barrier = pltpu.get_barrier_semaphore()
    for target in targets:
        pl.semaphore_signal(barrier, inc=1, device_id=target, device_id_type=MESH)
    pl.semaphore_wait(barrier, len(targets))


def when(condition, action):
    if condition is None:
        action()
    else:
        pl.when(condition)(action)


class PlaneGather:
    SENT = (
        (0, 0, 1, 1, None), (0, 0, 1, -1, None), (-1, 0, 1, 1, 0), (1, 0, 1, -1, 1),
        (0, 0, 0, 1, None), (-1, 0, 0, 1, None), (1, 0, 0, 1, None), (2, 0, 0, 1, None),
        (0, 0, 0, -1, None), (-1, 0, 0, -1, None), (1, 0, 0, -1, None), (2, 0, 0, -1, None),
        (0, -1, 0, 1, None), (-1, -1, 0, 1, None), (1, 1, 0, -1, None), (2, 1, 0, -1, None),
    )
    GOT = (
        (-1, 0, None), (1, 0, None), (2, 0, 0), (2, 0, 1),
        (0, -1, None), (-1, -1, None), (1, -1, None), (2, -1, None),
        (0, 1, None), (-1, 1, None), (1, 1, None), (2, 1, None),
        (0, 2, None), (-1, 2, None), (1, 2, None), (2, 2, None),
    )
    EVENTS = (
        ((0,), (2, 5, 9)), ((1,), (3, 6, 10)), ((4,), (12,)), ((8,), ()), ((2, 3), (7, 11)), ((5,), (13,)), ((10,), (14,)),
        ((9,), ()), ((6,), ()), ((11,), (15,)), ((7,), ()), ((12,), ()), ((13,), ()), ((14,), ()), ((15,), ()),
    )
    PLACES = tuple(((-1, 0), (1, 0), (0, -1), (0, 1), (2, 0), (-1, -1), (1, 1), (-1, 1), (1, -1), (2, 1), (2, -1), (0, 2), (-1, 2), (1, 2), (2, 2)))

    def __init__(self, buf, rows, send, recv, pos, only=None):
        self.buf, self.rows, self.send, self.recv, self.pos, self.only = buf, rows, send, recv, pos, only

    def block(self, half, first, second):
        dx, dy = (second, first) if half == 0 else (first, second)
        return lax.rem(self.pos[0] + dx % 4, 4), lax.rem(self.pos[1] + dy % 4, 4)

    def piece(self, half, first, second, part=None):
        size = self.rows // 2
        start = half * size
        if part is not None:
            size //= 2
            start += part * size
        bx, by = self.block(half, first, second)
        return self.buf.at[bx, by, pl.ds(start, size)]

    def cond(self, half, first, second):
        return None if self.only is None else self.only(*self.block(half, first, second))

    def copy(self, half, kind, first, second, axis, step, part=None):
        axis = axis if half == 0 else 1 - axis
        ref = self.piece(half, first, second, part)
        return remote(ref, ref, self.send.at[half, kind], self.recv.at[half, kind], moved(self.pos, axis, step))

    def go(self, half, kind):
        first, second, axis, step, part = self.SENT[kind]
        when(self.cond(half, first, second), lambda: self.copy(half, kind, first, second, axis, step, part).start())

    def arrive(self, half, kind):
        first, second, part = self.GOT[kind]
        when(self.cond(half, first, second), lambda: self.copy(half, kind, first, second, 0, 1, part).wait_recv())

    def begin(self):
        for kind in (0, 1, 4, 8):
            for half in (0, 1):
                self.go(half, kind)

    def event(self, number, half):
        kinds, on = self.EVENTS[number]
        for kind in kinds:
            self.arrive(half, kind)
        for kind in on:
            self.go(half, kind)

    def finish(self):
        for half in (0, 1):
            for kind in range(16):
                first, second, axis, step, part = self.SENT[kind]
                when(
                    self.cond(half, first, second),
                    lambda: self.copy(half, kind, first, second, axis, step, part).wait_send(),
                )


class ColumnGather:
    def __init__(self, buf, send, recv, pos):
        self.buf, self.send, self.recv, self.pos = buf, send, recv, pos

    def piece(self, dz, dk=0, part=None):
        z, k = self.pos[2], self.pos[3]
        slot = lax.rem(z + dz % 4, 4) * 2 + lax.rem(k + dk, 2)
        if part is None:
            return self.buf.at[slot]
        return self.buf.at[slot, pl.ds(32 * part, 32)]

    SENT = {0: (0, 2, 1, None), 1: (0, 2, -1, None), 2: (-1, 2, 1, 0), 3: (1, 2, -1, 1),
            4: (0, 3, 1, None), 5: (-1, 3, 1, None), 6: (1, 3, 1, None), 7: (2, 3, 1, None)}
    GOT = {0: (-1, 0, None), 1: (1, 0, None), 2: (2, 0, 0), 3: (2, 0, 1),
           4: (0, 1, None), 5: (-1, 1, None), 6: (1, 1, None), 7: (2, 1, None)}

    def go(self, kind):
        dz, axis, step, part = self.SENT[kind]
        ref = self.piece(dz, 0, part)
        remote(ref, ref, self.send.at[kind], self.recv.at[kind], moved(self.pos, axis, step)).start()

    def arrive(self, kind):
        dz, dk, part = self.GOT[kind]
        ref = self.piece(dz, dk, part)
        remote(ref, ref, self.send.at[kind], self.recv.at[kind], moved(self.pos, 2, 1)).wait_recv()

    def begin(self):
        for kind in (0, 1, 4):
            self.go(kind)

    def middle(self):
        self.arrive(0)
        self.go(2)
        self.go(5)
        self.arrive(1)
        self.go(3)
        self.go(6)

    def end(self):
        self.arrive(2)
        self.arrive(3)
        self.go(7)
        for kind in (4, 5, 6, 7):
            self.arrive(kind)

    def finish(self):
        for kind in range(8):
            dz, axis, step, part = self.SENT[kind]
            ref = self.piece(dz, 0, part)
            remote(ref, ref, self.send.at[kind], self.recv.at[kind], moved(self.pos, axis, step)).wait_send()


def column_peers(pos):
    peers = []
    for dz in range(4):
        for dk in range(2):
            if dz or dk:
                peers.append(moved(moved(pos, 2, dz), 3, dk))
    return peers


def to_all_columns(buf, send, recv, pos):
    copies = []
    mine = pos[2] * 2 + pos[3]
    number = 0
    for dz in range(4):
        for dk in range(2):
            if dz == 0 and dk == 0:
                continue
            target = moved(moved(pos, 2, dz), 3, dk)
            out = remote(buf.at[mine], buf.at[mine], send.at[number], recv.at[number], target)
            origin = moved(moved(pos, 2, -dz), 3, -dk)
            slot = origin[2] * 2 + origin[3]
            into = remote(buf.at[slot], buf.at[slot], send.at[number], recv.at[number], target)
            copies.append((out, into))
            number += 1
    return copies


def to_axis(buf, send, recv, pos, axis):
    copies = []
    mine = pos[axis]
    for step in (1, 2, 3):
        target = moved(pos, axis, step)
        out = remote(buf.at[mine], buf.at[mine], send.at[step - 1], recv.at[step - 1], target)
        slot = moved(pos, axis, -step)[axis]
        into = remote(buf.at[slot], buf.at[slot], send.at[step - 1], recv.at[step - 1], target)
        copies.append((out, into))
    return copies


def exchange(copies):
    for out, _ in copies:
        out.start()
    for _, into in copies:
        into.wait_recv()


def split(value):
    high = value.astype(BF16)
    return high, (value - high.astype(F32)).astype(BF16)


def dot3(left, right, dims):
    lh, ll = split(left)
    rh, rl = split(right)
    dot = functools.partial(lax.dot_general, dimension_numbers=(dims, ((), ())), preferred_element_type=F32)
    return dot(lh, rh) + (dot(lh, rl) + dot(ll, rh))


def small_factor(work, extra):
    lane = lax.broadcasted_iota(jnp.int32, (1, 128), 1)

    def body(step, carry):
        start = pl.multiple_of(step * BASE, BASE)
        rows = work[pl.ds(start, BASE), :]
        turned = pltpu.roll(rows[:, :128], lax.rem(128 - start, 128), 1)
        entry = [[jnp.broadcast_to(turned[i : i + 1, j : j + 1], (1, 128)) for j in range(i + 1)] for i in range(BASE)]
        solved = []
        for j in range(BASE):
            inverse = lax.rsqrt(entry[j][j])
            row = rows[j : j + 1, :]
            for m in range(j):
                row = row - jnp.concatenate([entry[j][m]] * 2, axis=1) * solved[m]
            solved.append(row * jnp.concatenate([inverse] * 2, axis=1))
            for i in range(j + 1, BASE):
                entry[i][j] = entry[i][j] * inverse
            for i in range(j + 1, BASE):
                for m in range(j + 1, i + 1):
                    entry[i][m] = entry[i][m] - entry[i][j] * entry[m][j]
        block = jnp.concatenate(solved, axis=0)
        work[pl.ds(start, BASE), :] = block
        later = jnp.where(lane >= start + BASE, block[:, :128], 0.0)
        lh, ll = split(later)
        rh, rl = split(block)
        left = jnp.concatenate([lh, lh, ll], axis=0)
        right = jnp.concatenate([rh, rl, rh], axis=0)
        work[...] = work[...] - lax.dot_general(left, right, (((0,), (0,)), ((), ())), preferred_element_type=F32)
        for number, action in extra.items():
            pl.when(step == number)(action)
        return carry

    lax.fori_loop(0, 128 // BASE, body, 0)


def factor(aug, work, extras):
    eye = (lax.broadcasted_iota(jnp.int32, (128, 128), 0) == lax.broadcasted_iota(jnp.int32, (128, 128), 1)).astype(F32)
    for number in range(4):
        lo, hi = number * 128, (number + 1) * 128
        work[:, 0:128] = aug[lo:hi, lo:hi]
        work[:, 128:256] = eye
        small_factor(work, extras[number])
        inverse = work[:, 128:256]
        if hi < 512:
            right = dot3(inverse, aug[lo:hi, hi : 512 + lo], ((1,), (0,)))
            full = jnp.concatenate([right, inverse], axis=1)
            aug[lo:hi, hi : 512 + hi] = full
            ahead = right[:, 0 : 512 - hi]
            aug[hi:512, hi : 512 + hi] = aug[hi:512, hi : 512 + hi] - dot3(ahead, full, ((0,), (0,)))
        else:
            aug[lo:hi, 512 : 512 + lo] = dot3(inverse, aug[lo:hi, 512 : 512 + lo], ((1,), (0,)))
            aug[lo:hi, 512 + lo : 512 + hi] = inverse


def panel_kernel(
    subject_ref, gain_ref, gate_ref, up_ref, cov_ref, kc_out, kr_out, k5_out, cr_out, cc_out, inv_ref, scale_ref,
    kc, kr, k5, k5_scaled, cr, cc, first, jj, aug, work,
    xx, own_w, other_w, sel_w, squares, part, hop_out, hop_in, total, sum_y, sum_x, sum_c, cov_rows, cov_cols,
    local_sem, w_send, w_recv, sq_send, sq_recv, x_send, x_recv, sib_send, sib_recv,
    hop_send, hop_recv, sy_send, sy_recv, sx_send, sx_recv, sc_send, sc_recv, cc_send, cc_recv,
    kc_send, kc_recv, k5_send, k5_recv, cr_send, cr_recv, jj_send, jj_recv, f_send, f_recv, row_send, row_recv, out_sem,
):
    pos = here()
    x, y, z, k = pos
    sibling = moved(pos, 3, 1)
    col = z * 2 + k
    plane = [moved(pos, axis, step) for axis in (0, 1) for step in (1, 2, 3)]
    greet(plane + column_peers(pos))

    weights = ((gate_ref, 0), (up_ref, 1))

    def swap(ref, index):
        return remote(ref, other_w.at[index], w_send.at[index], w_recv.at[index], sibling)

    def fetch(ref, index):
        return pltpu.make_async_copy(ref, own_w.at[index], local_sem.at[index])

    fetch_rows = pltpu.make_async_copy(cov_ref.at[pl.ds(0, 64)], cov_rows, local_sem.at[2])
    fetch_cols = pltpu.make_async_copy(cov_ref.at[:, pl.ds(0, 128)], cov_cols, local_sem.at[3])

    subject = subject_ref[...].astype(F32)
    squared = subject * subject
    folded = squared[:, 0:128]
    for group in range(1, 5):
        folded = folded + squared[:, group * 128 : (group + 1) * 128]
    squares[col] = folded
    square_copies = to_all_columns(squares, sq_send, sq_recv, pos)
    for out, _ in square_copies:
        out.start()
    for ref, index in weights:
        fetch(ref, index).start()
        swap(ref, index).start()
    fetch_rows.start()
    fetch_cols.start()

    def select(source, core):
        def body(step, carry):
            for index in range(2):
                low = source[index, :, pl.ds(pl.multiple_of(step * 128, 128), 128)]
                high = source[index, :, pl.ds(pl.multiple_of(512 + step * 128, 128), 128)]

                @pl.when(k == 0)
                def _():
                    sel_w[step, pl.ds(pl.multiple_of(core * 640, 128), 640), pl.ds(index * 128, 128)] = jnp.concatenate(
                        [low[:, :64], high[:, :64]], axis=1
                    )

                @pl.when(k == 1)
                def _():
                    sel_w[step, pl.ds(pl.multiple_of(core * 640, 128), 640), pl.ds(index * 128, 128)] = jnp.concatenate(
                        [low[:, 64:], high[:, 64:]], axis=1
                    )

            return carry

        lax.fori_loop(0, 4, body, 0)

    for _, into in square_copies:
        into.wait_recv()
    everyone = squares[0]
    for member in range(1, 8):
        everyone = everyone + squares[member]
    inverse_rms = lax.rsqrt(jnp.sum(everyone, axis=1, keepdims=True) / WIDTH + EPSILON)
    xx[k, x, y] = (subject * inverse_rms * gain_ref[...]).astype(BF16)

    gather = PlaneGather(xx.at[k], 64, x_send, x_recv, pos)
    gather.begin()

    def to_sibling(half, number, first, second):
        ref = gather.piece(half, first, second)
        return remote(ref, ref, sib_send.at[half, number], sib_recv.at[half, number], sibling)

    def from_sibling(half, number, first, second):
        bx, by = gather.block(half, first, second)
        ref = xx.at[1 - k, bx, by, pl.ds(half * 32, 32)]
        return remote(ref, ref, sib_send.at[half, number], sib_recv.at[half, number], sibling)

    places = ((0, 0),) + PlaneGather.PLACES
    for half in (0, 1):
        to_sibling(half, 0, 0, 0).start()

    for ref, index in weights:
        fetch(ref, index).wait()
    select(own_w, k)

    def arrivals(numbers):
        for number in numbers:
            for half in (0, 1):
                gather.event(number, half)
                to_sibling(half, number + 1, *places[number + 1]).start()

    def siblings(numbers):
        for number in numbers:
            for half in (0, 1):
                from_sibling(half, number, *places[number]).wait_recv()

    def line(core, half, second):
        if half == 0:
            value = xx[core, lax.rem(x + second % 4, 4), :, 0:32, :]
        else:
            value = xx[core, :, lax.rem(y + second % 4, 4), 32:64, :]
        return value.reshape(128, 640)

    def product(chunk, dest):
        second = (0, -1, 1, 2)[chunk]
        value = None
        for core in (0, 1):
            left = jnp.concatenate([line(core, 0, second), line(core, 1, second)], axis=0)
            term = jnp.dot(left, sel_w[dest, core * 640 : core * 640 + 640], preferred_element_type=F32)
            value = term if value is None else value + term
        return value

    def dest(step):
        return lax.rem(z + step % 4, 4)

    def hop(chunk, kind):
        target = moved(pos, 2, 1 if kind % 2 == 0 else -1)
        return remote(
            hop_out.at[chunk, kind], hop_in.at[chunk, kind], hop_send.at[chunk, kind], hop_recv.at[chunk, kind], target
        )

    def send(chunk, kind, value):
        hop_out[chunk, kind] = value.astype(BF16)
        hop(chunk, kind).start()

    def multiply(chunk):
        value = product(chunk, dest(2))
        send(chunk, 0, value[:128])
        send(chunk, 1, value[128:])
        value = product(chunk, dest(1))
        send(chunk, 2, value[128:])
        part[chunk, 0] = value[:128]
        value = product(chunk, dest(-1))
        send(chunk, 3, value[:128])
        part[chunk, 1] = value[128:]
        value = product(chunk, dest(0))
        part[chunk, 2] = value[:128]
        part[chunk, 3] = value[128:]

    def join(chunk):
        hop(chunk, 0).wait_recv()
        send(chunk, 4, part[chunk, 0] + hop_in[chunk, 0].astype(F32))
        hop(chunk, 1).wait_recv()
        send(chunk, 5, part[chunk, 1] + hop_in[chunk, 1].astype(F32))

    def finish(chunk):
        second = (0, -1, 1, 2)[chunk]
        for half in (0, 1):
            kinds = (4, 3) if half == 0 else (2, 5)
            for kind in kinds:
                hop(chunk, kind).wait_recv()
            value = part[chunk, 2 + half] + (hop_in[chunk, kinds[0]].astype(F32) + hop_in[chunk, kinds[1]].astype(F32))
            gate, up = value[:, :128], value[:, 128:]
            raw = gate / (1.0 + jnp.exp(-gate)) * up
            place = lax.rem((x if half == 0 else y) + second % 4, 4)
            total[:, pl.ds(pl.multiple_of(half * 512 + place * 128, 128), 128)] = raw.T

    covs = PlaneGather(cc, 64, cc_send, cc_recv, pos, only=lambda bx, by: bx < 2)

    def cov_events(numbers):
        for number in numbers:
            for half in (0, 1):
                covs.event(number, half)

    arrivals((0, 1, 4))
    for ref, index in weights:
        swap(ref, index).wait_recv()
    select(other_w, 1 - k)
    arrivals((2, 3))
    siblings((0, 1, 2, 5))
    multiply(0)
    arrivals((5, 8, 10))
    siblings((3, 6, 9, 11))
    multiply(1)
    join(0)
    arrivals((6, 7, 9))
    siblings((4, 7, 8, 10))
    multiply(2)
    join(1)
    arrivals((11, 12, 13, 14))

    fetch_rows.wait()

    @pl.when(x < 2)
    def _():
        cc[x, y] = cov_rows[...].astype(BF16)

    covs.begin()
    siblings((12, 13, 14, 15))
    multiply(3)
    join(2)
    fetch_cols.wait()
    cr[col] = cov_cols[...].T[0:64].astype(BF16)
    cov_events((0, 1))
    finish(0)
    cov_events((2, 3, 4))
    join(3)
    finish(1)
    cov_events((5, 6))
    finish(2)
    cov_events((7, 8, 9))
    finish(3)
    raw = total[...]
    mass = jnp.sum(raw * raw, axis=0, keepdims=True)
    own_keys = raw.astype(BF16)
    row = x * 4 + y

    @pl.when(row == 0)
    def _():
        first[0, 0] = own_keys[0:64]

    first_tile = PlaneGather(first, 64, f_send, f_recv, pos, only=lambda bx, by: (bx == 0) & (by == 0))
    first_tile.begin()
    sum_y[y] = jnp.broadcast_to(mass, (8, PROMPTS))
    y_copies = to_axis(sum_y, sy_send, sy_recv, pos, 1)
    for out, _ in y_copies:
        out.start()
    kc[x, y] = own_keys
    keys = PlaneGather(kc, 128, kc_send, kc_recv, pos)
    keys.begin()
    cov_events((10, 11, 12, 13, 14))
    jj[col] = cc[:, :, :, 0:128].reshape(512, 128).astype(F32).T[0:64].astype(BF16)
    corner = ColumnGather(jj, jj_send, jj_recv, pos)
    corner.begin()
    for _, into in y_copies:
        into.wait_recv()
    sum_x[x] = sum_y[0] + sum_y[1] + sum_y[2] + sum_y[3]
    x_copies = to_axis(sum_x, sx_send, sx_recv, pos, 0)
    for out, _ in x_copies:
        out.start()

    def first_events(numbers):
        for number in numbers:
            first_tile.event(number, 0)
            first_tile.event(number, 1)

    first_events((0, 1, 2, 3))
    for _, into in x_copies:
        into.wait_recv()
    sum_c[col] = sum_x[0] + sum_x[1] + sum_x[2] + sum_x[3]
    c_copies = to_all_columns(sum_c, sc_send, sc_recv, pos)
    for out, _ in c_copies:
        out.start()
    first_events(range(4, 15))
    k5[col] = first[0, 0]
    first_keys = ColumnGather(k5, k5_send, k5_recv, pos)
    first_keys.begin()

    source = lax.rem(row, 8)
    source_z = source // 2
    upper = row // 8
    away = lax.rem(z + 4 - source_z, 4)
    same = k == lax.rem(source, 2)

    def wave(number, kind, own=False):
        one, two = keys.block(0, *places[number]), keys.block(1, *places[number])
        bx = jnp.where(upper == 0, one[0], two[0])
        by = jnp.where(upper == 0, one[1], two[1])
        part = kind % 2
        dst = kr.at[bx, by, pl.ds(part * 32, 32)]
        src = kc.at[bx, by, pl.ds(pl.multiple_of(upper * 64 + part * 32, 32), 32)] if own else dst
        target = sibling if kind >= 2 else moved(pos, 2, 1 if kind == 0 else -1)
        return remote(src, dst, row_send.at[number, kind], row_recv.at[number, kind], target)

    def own_copy(number):
        one, two = keys.block(0, *places[number]), keys.block(1, *places[number])
        bx = jnp.where(upper == 0, one[0], two[0])
        by = jnp.where(upper == 0, one[1], two[1])
        return pltpu.make_async_copy(
            kc.at[bx, by, pl.ds(pl.multiple_of(upper * 64, 64), 64)], kr.at[bx, by], out_sem.at[number]
        )

    def relay(number):
        if number < 16:

            @pl.when(same & (away == 0))
            def _():
                for kind in (0, 1, 2, 3):
                    wave(number, kind, own=True).start()
                own_copy(number).start()

        for distance in (1, 2, 3):
            for kind, hops in ((0, distance), (1, 4 - distance)):
                block = number - LAG * hops
                if 0 <= block < 16:

                    @pl.when(same & (away == distance))
                    def _():
                        wave(block, kind).wait_recv()
                        if hops < 3:
                            wave(block, kind).start()
                        wave(block, kind + 2).start()

    def key_event(number):
        if number < 15:
            keys.event(number, 0)
            keys.event(number, 1)
        relay(number + 1)

    panel_rows = ColumnGather(cr, cr_send, cr_recv, pos)
    corner.middle()
    relay(0)
    key_event(0)
    for _, into in c_copies:
        into.wait_recv()
    mass = sum_c[0]
    for member in range(1, 8):
        mass = mass + sum_c[member]
    scale = lax.rsqrt(mass / HIDDEN + EPSILON) * (1.0 / 32.0)
    scale_ref[...] = scale * scale
    first_keys.middle()
    corner.end()
    key_event(1)
    first_keys.end()
    panel_rows.begin()
    key_event(2)

    def save(number, source, target):
        return pltpu.make_async_copy(source, target, out_sem.at[16 + number])

    corner_raw = k5[...].reshape(512, PROMPTS).astype(F32)
    corner_keys = (corner_raw * scale[0:1]).astype(BF16)
    outer = lax.dot_general(corner_keys, corner_keys, (((1,), (1,)), ((), ())), preferred_element_type=F32)
    aug[:, 0:512] = jj[...].reshape(512, 512).astype(F32) + outer
    aug[:, 512:1024] = (
        lax.broadcasted_iota(jnp.int32, (512, 512), 0) == lax.broadcasted_iota(jnp.int32, (512, 512), 1)
    ).astype(F32)
    k5_scaled[...] = (corner_raw * (scale * scale)[0:1]).astype(BF16).reshape(8, 64, PROMPTS)
    save(0, k5_scaled, k5_out).start()
    save(1, cc, cc_out).start()
    beside = {
        3: 0, 4: 1, 5: 3, 6: 5, 7: 7, 8: 9, 9: 11, 10: 13, 11: 15, 12: 17, 13: 19, 14: 21, 15: 23, 16: 24, 17: 25, 18: 26, 19: 28, 20: 30,
    }
    extras = [{} for _ in range(4)]
    for number, step in beside.items():
        extras[step // 8][step % 8] = functools.partial(key_event, number)
    extras[0][2] = panel_rows.middle
    extras[0][6] = panel_rows.end
    extras[2][6] = lambda: save(2, kc, kc_out).start()
    extras[2][4] = lambda: save(3, cr, cr_out).start()
    factor(aug, work, extras)
    inv_ref[...] = aug[:, 512:1024]

    for number in range(16):

        @pl.when(k != lax.rem(source, 2))
        def _():
            wave(number, 2).wait_recv()
            wave(number, 3).wait_recv()

        @pl.when(same & (away == 0))
        def _():
            for kind in range(4):
                wave(number, kind, own=True).wait_send()
            own_copy(number).wait()

        for distance in (1, 2, 3):

            @pl.when(same & (away == distance))
            def _():
                for kind, hops in ((0, distance), (1, 4 - distance)):
                    if hops < 3:
                        wave(number, kind).wait_send()
                    wave(number, kind + 2).wait_send()

    first_tile.finish()
    keys.finish()
    panel_rows.finish()
    first_keys.finish()
    corner.finish()
    save(4, kr, kr_out).start()
    for ref, index in weights:
        swap(ref, index).wait_send()
    for copies in (square_copies, y_copies, x_copies, c_copies):
        for out, _ in copies:
            out.wait_send()
    gather.finish()
    covs.finish()
    for half in (0, 1):
        for number in range(16):
            to_sibling(half, number, *places[number]).wait_send()
    for chunk in range(4):
        for kind in range(6):
            hop(chunk, kind).wait_send()
    save(0, k5_scaled, k5_out).wait()
    save(1, cc, cc_out).wait()
    save(2, kc, kc_out).wait()
    save(3, cr, cr_out).wait()
    save(4, kr, kr_out).wait()


def panel(subject, gain, w_gate, w_up, cov):
    dma = pltpu.SemaphoreType.DMA
    vmem = pl.BlockSpec(memory_space=pltpu.VMEM)
    anywhere = pl.BlockSpec(memory_space=pl.ANY)
    spread = (
        ((4, 4, 128, PROMPTS), BF16),
        ((4, 4, 64, PROMPTS), BF16),
        ((8, 64, PROMPTS), BF16),
        ((8, 64, 1024), BF16),
        ((2, 4, 64, 2048), BF16),
    )
    return pl.pallas_call(
        panel_kernel,
        name="keys_and_panel",
        out_shape=tuple(jax.ShapeDtypeStruct(*one) for one in spread)
        + (jax.ShapeDtypeStruct((512, 512), F32), jax.ShapeDtypeStruct((8, PROMPTS), F32)),
        in_specs=[vmem] * 2 + [anywhere] * 3,
        out_specs=(anywhere,) * 5 + (vmem,) * 2,
        scratch_shapes=[
            pltpu.VMEM(*spread[0]), pltpu.VMEM(*spread[1]), pltpu.VMEM(*spread[2]), pltpu.VMEM(*spread[2]),
            pltpu.VMEM(*spread[3]), pltpu.VMEM(*spread[4]),
            pltpu.VMEM((1, 1, 64, PROMPTS), BF16),
            pltpu.VMEM((8, 64, 512), BF16),
            pltpu.VMEM((512, 1024), F32),
            pltpu.VMEM((128, 256), F32),
            pltpu.VMEM((2, 4, 4, 64, 640), BF16),
            pltpu.VMEM((2, 640, 1024), BF16),
            pltpu.VMEM((2, 640, 1024), BF16),
            pltpu.VMEM((4, 1280, 256), BF16),
            pltpu.VMEM((8, 64, 128), F32),
            pltpu.VMEM((4, 4, 128, 256), F32),
            pltpu.VMEM((4, 6, 128, 256), BF16),
            pltpu.VMEM((4, 6, 128, 256), BF16),
            pltpu.VMEM((128, PROMPTS), F32),
            pltpu.VMEM((4, 8, PROMPTS), F32),
            pltpu.VMEM((4, 8, PROMPTS), F32),
            pltpu.VMEM((8, 8, PROMPTS), F32),
            pltpu.VMEM((64, 2048), F32),
            pltpu.VMEM((1024, 128), F32),
            dma((4,)), dma((2,)), dma((2,)), dma((7,)), dma((7,)), dma((2, 16)), dma((2, 16)), dma((2, 16)), dma((2, 16)),
            dma((4, 6)), dma((4, 6)), dma((3,)), dma((3,)), dma((3,)), dma((3,)), dma((7,)), dma((7,)), dma((2, 16)), dma((2, 16)),
            dma((2, 16)), dma((2, 16)), dma((8,)), dma((8,)), dma((8,)), dma((8,)), dma((8,)), dma((8,)), dma((2, 16)), dma((2, 16)),
            dma((16, 4)), dma((16, 4)), dma((21,)),
        ],
        compiler_params=pltpu.CompilerParams(collective_id=0, has_side_effects=True, vmem_limit_bytes=VMEM_LIMIT),
    )(subject, gain, w_gate, w_up, cov)


def update_kernel(cov_ref, kc_ref, kr_ref, k5_ref, cr_ref, cc_ref, inv_ref, scale_ref, out_ref, covb, outb, panel, in_sem, out_sem):
    x, y, z, k = here()
    row = x * 4 + y
    col = z * 2 + k
    nt = (((1,), (1,)), ((), ()))
    nn = (((1,), (0,)), ((), ()))
    tn = (((0,), (0,)), ((), ()))
    dot = functools.partial(lax.dot_general, preferred_element_type=F32)

    def load(step):
        area = (pl.ds(step * 128, 1024 - step * 128), pl.ds(step * 256, 256))
        return pltpu.make_async_copy(cov_ref.at[area], covb.at[step % 2, pl.ds(step * 128, 1024 - step * 128)], in_sem.at[step % 2])

    def store(step):
        return pltpu.make_async_copy(outb.at[step % 2], out_ref.at[:, pl.ds(step * 256, 256)], out_sem.at[step % 2])

    load(0).start()
    load(1).start()
    inverse = inv_ref[...]
    inverse_high = inverse.astype(BF16)
    first = k5_ref[...].reshape(512, PROMPTS)
    raw_rows = kr_ref[...].reshape(1024, PROMPTS)
    rows = (raw_rows.astype(F32) * scale_ref[0:1]).astype(BF16)
    matrix_rows = cr_ref[...].reshape(512, 1024).astype(F32) + dot(first, raw_rows, nt)
    high, low = split(matrix_rows)
    panel[...] = dot(inverse_high, high, nn)
    own = inv_ref[pl.ds(pl.multiple_of(col * 64, 64), 64), :]
    own_high, own_low = split(own)
    own_panel = dot(own_high, high, nn) + (dot(own_low, high, nn) + dot(own_high, low, nn))
    panel_low = panel[...].astype(BF16)
    for step in range(8):
        top = step * 128
        height = 1024 - top
        load(step).wait()
        if step >= 2:
            store(step - 2).wait()
        cols = kc_ref[2 * step : 2 * step + 2].reshape(256, PROMPTS)
        matrix_cols = cc_ref[:, :, step * 256 : (step + 1) * 256].reshape(512, 256).astype(F32) + dot(first, cols, nt)
        panel_cols = dot(inverse_high, matrix_cols.astype(BF16), nn).astype(BF16)
        value = covb[step % 2, top:1024] + dot(rows[top:], cols, nt) - dot(panel_low[:, top:], panel_cols, tn)
        if step == 0:
            value = jnp.concatenate([own_panel.T, value[:, 64:]], axis=1)
        i = lax.broadcasted_iota(jnp.int32, (height, 256), 0) + top
        j = lax.broadcasted_iota(jnp.int32, (height, 256), 1) + step * 256
        row_global = (i // 64 * 16 + row) * 64 + i % 64
        col_global = (j // 64 * 8 + col) * 64 + j % 64
        outb[step % 2, top:1024] = jnp.where(row_global >= col_global, value, 0.0)
        if step:
            outb[step % 2, 0:top] = jnp.zeros((top, 256), F32)
        store(step).start()
        if step + 2 < 8:
            load(step + 2).start()
    store(6).wait()
    store(7).wait()


def update(cov, kc, kr, k5, cr, cc, inverse, scale):
    dma = pltpu.SemaphoreType.DMA
    vmem = pl.BlockSpec(memory_space=pltpu.VMEM)
    return pl.pallas_call(
        update_kernel,
        name="update_lower",
        out_shape=jax.ShapeDtypeStruct((1024, 2048), F32),
        in_specs=[pl.BlockSpec(memory_space=pl.ANY)] + [vmem] * 7,
        out_specs=pl.BlockSpec(memory_space=pl.ANY),
        scratch_shapes=[
            pltpu.VMEM((2, 1024, 256), F32), pltpu.VMEM((2, 1024, 256), F32), pltpu.VMEM((512, 1024), F32), dma((2,)), dma((2,)),
        ],
        compiler_params=pltpu.CompilerParams(vmem_limit_bytes=VMEM_LIMIT),
    )(cov, kc, kr, k5, cr, cc, inverse, scale)


def on_device(residual, positions, norm_gain, w_gate, w_up, covariance):
    prompts, tokens, _ = residual.shape
    token = lax.broadcasted_iota(jnp.int32, (prompts, tokens), 1)
    picked = jnp.where((token == positions[:, None])[:, :, None], residual, jnp.zeros_like(residual))
    subject = jnp.sum(picked.astype(F32), axis=1).astype(BF16)
    kc, kr, k5, cr, cc, inverse, scale = panel(subject, norm_gain[None, :], w_gate, w_up, covariance)
    kc = kc.reshape(16, 128, PROMPTS)
    kr = kr.reshape(16, 64, PROMPTS)
    cc = cc.reshape(8, 64, 2048)
    return update(covariance, kc, kr, k5, cr, cc, inverse, scale)


def solution(mesh):
    torus = Mesh(mesh.devices.reshape(4, 4, 4, 2), ("x", "y", "z", "k"))
    row, col = ("x", "y"), ("z", "k")
    placed = (P(row, None, col), P(row), P(col), P(col, row), P(col, row), P(row, col))
    return jax.shard_map(on_device, mesh=torus, in_specs=placed, out_specs=P(row, col), check_vma=False)
```

time: 191 us -> 150 us (0.79)
  Pallas kernels: 186 us -> 145 us
    pallas_call x2 -> x1, Pallas kernels: 165 us -> 124 us  [panel(): pl.pallas_call(panel_kernel, name='keys_and_panel', out_shape=tuple((jax....]
where the time goes in v3:
time: 150 us
  Pallas kernels  145 us (97%)
  other arithmetic  3.25 us (2%)
    pallas_call x1, Pallas kernels, panel(): pl.pallas_call(panel_kernel, name='keys_and_panel', out_shape=tuple((jax....  124 us
    pallas_call x1, Pallas kernels, update(): pl.pallas_call(update_kernel, name='update_lower', out_shape=jax.ShapeDty...  20.6 us

profile of v3, /device:TPU:20, one launch (start us, length us, event | category | flops | bytes accessed | tf_op | source)
XLA Modules:
  0.0 149.6 jit_solution(713167424306539352)
XLA Ops:
  0.0 1.3 broadcast_in_dim.18.gain_ref
  1.3 0.7 iota_compare_fusion
  2.0 2.5 %select_reduce_fusion.subject_ref = bf16[64,640]{1,0:T(8,128)(2,1)} fusion(bf16[64,16,640]{2,1,0:T(8,128)(2,1)} %param.6, pred[64,16]{1,0:T(8,128)(4,1)S(1)} %iota_compare_fusion), kind=kLoop, calls=%fused_computation | loop fusion | flops 1269760 | bytes 1393664 | tf_op jit(solution)/shard_map/reduce_sum | solution.py:812
  4.5 124.2 %keys_and_panel.1 = (bf16[4,4,128,1024]{3,2,1,0:T(8,128)(2,1)}, bf16[4,4,64,1024]{3,2,1,0:T(8,128)(2,1)}, bf16[8,64,1024]{2,1,0:T(8,128)(2,1)}, bf16[8,64,1024]{...) custom-call(bf16[64,640]{1,0:T(8,128)(2,1)} %select_reduce_fusion.subject_ref, ...), custom_call_target="tpu_custom_call" | custom-call | tf_op jit(solution)/shard_map/keys_and_panel/pallas_call | solution.py:699
  128.8 20.6 %update_lower.1 = f32[1024,2048]{1,0:T(8,128)} custom-call(f32[1024,2048]{1,0:T(8,128)} %cov_ref.3, bf16[16,128,1024]{2,1,0:T(8,128)(2,1)} %bitcast.3, bf16[16,64,1024]{2,1,0:T(8,128)(2,1)} %bitcast.4, bf16[8,64,1024]{2,1,0:T(8,128)(2,1)} %get-tuple-element.14.k5_ref, bf16[8,64,1024]{2,1,0:T(8,128)(2,1)} %get-tuple-element.15.cr_ref, ...), custom_call_target="tpu_custom_call" | custom-call | tf_op jit(solution)/shard_map/update_lower/pallas_call | solution.py:795

commit v4 on v3

--- a/solution.py
+++ b/solution.py
@@ -289,19 +289,22 @@
 
 
 def panel_kernel(
-    subject_ref, gain_ref, gate_ref, up_ref, cov_ref, kc_out, kr_out, k5_out, cr_out, cc_out, inv_ref, scale_ref,
+    residual_ref, positions_ref, gain_ref, gate_ref, up_ref, cov_ref, kc_out, kr_out, k5_out, cr_out, cc_out, inv_ref, scale_ref,
     kc, kr, k5, k5_scaled, cr, cc, first, jj, aug, work,
-    xx, own_w, other_w, sel_w, squares, part, hop_out, hop_in, total, sum_y, sum_x, sum_c, cov_rows, cov_cols,
+    xx, own_w, other_w, sel_w, squares, part, hop_out, hop_in, total, sum_y, sum_x, sum_c, cov_rows, cov_cols, cov_corner, tiles,
     local_sem, w_send, w_recv, sq_send, sq_recv, x_send, x_recv, sib_send, sib_recv,
     hop_send, hop_recv, sy_send, sy_recv, sx_send, sx_recv, sc_send, sc_recv, cc_send, cc_recv,
-    kc_send, kc_recv, k5_send, k5_recv, cr_send, cr_recv, jj_send, jj_recv, f_send, f_recv, row_send, row_recv, out_sem,
+    kc_send, kc_recv, k5_send, k5_recv, cr_send, cr_recv, jj_send, jj_recv, f_send, f_recv, row_send, row_recv, out_sem, tile_send, tile_recv,
 ):
     pos = here()
     x, y, z, k = pos
     sibling = moved(pos, 3, 1)
     col = z * 2 + k
     plane = [moved(pos, axis, step) for axis in (0, 1) for step in (1, 2, 3)]
-    greet(plane + column_peers(pos))
+    barrier = pltpu.get_barrier_semaphore()
+    peers = plane + column_peers(pos)
+    for peer in peers:
+        pl.semaphore_signal(barrier, inc=1, device_id=peer, device_id_type=MESH)
 
     weights = ((gate_ref, 0), (up_ref, 1))
 
@@ -314,18 +317,41 @@
     fetch_rows = pltpu.make_async_copy(cov_ref.at[pl.ds(0, 64)], cov_rows, local_sem.at[2])
     fetch_cols = pltpu.make_async_copy(cov_ref.at[:, pl.ds(0, 128)], cov_cols, local_sem.at[3])
 
-    subject = subject_ref[...].astype(F32)
+    fetch_corner = pltpu.make_async_copy(cov_ref.at[pl.ds(0, 64), pl.ds(0, 128)], cov_corner, local_sem.at[4])
+    fetch_corner.start()
+    line_of = lax.broadcasted_iota(jnp.int32, (64, 64), 0)
+    prompt_of = lax.broadcasted_iota(jnp.int32, (64, 64), 1)
+    place = positions_ref[...].reshape(1, 64).astype(F32)
+    place = jnp.sum(jnp.where(line_of == prompt_of, place, 0.0), axis=1, keepdims=True)
+    token = lax.broadcasted_iota(jnp.int32, (64, 1024), 1) - 16 * lax.broadcasted_iota(jnp.int32, (64, 1024), 0)
+    pick = (token.astype(F32) == place).astype(BF16)
+    subject = jnp.dot(pick, residual_ref[...].reshape(1024, 640), preferred_element_type=F32)
     squared = subject * subject
     folded = squared[:, 0:128]
     for group in range(1, 5):
         folded = folded + squared[:, group * 128 : (group + 1) * 128]
     squares[col] = folded
+    pl.semaphore_wait(barrier, len(peers))
     square_copies = to_all_columns(squares, sq_send, sq_recv, pos)
     for out, _ in square_copies:
         out.start()
     for ref, index in weights:
         fetch(ref, index).start()
         swap(ref, index).start()
+    fetch_corner.wait()
+
+    @pl.when(x < 2)
+    def _():
+        tiles[x, y] = cov_corner[...].astype(BF16)
+
+    corner_tiles = PlaneGather(tiles, 64, tile_send, tile_recv, pos, only=lambda bx, by: bx < 2)
+    corner_tiles.begin()
+
+    def tile_events(numbers):
+        for number in numbers:
+            for half in (0, 1):
+                corner_tiles.event(number, half)
+
     fetch_rows.start()
     fetch_cols.start()
 
@@ -357,7 +383,7 @@
     for member in range(1, 8):
         everyone = everyone + squares[member]
     inverse_rms = lax.rsqrt(jnp.sum(everyone, axis=1, keepdims=True) / WIDTH + EPSILON)
-    xx[k, x, y] = (subject * inverse_rms * gain_ref[...]).astype(BF16)
+    xx[k, x, y] = (subject * inverse_rms * gain_ref[...].reshape(1, 640)).astype(BF16)
 
     gather = PlaneGather(xx.at[k], 64, x_send, x_recv, pos)
     gather.begin()
@@ -458,21 +484,28 @@
             for half in (0, 1):
                 covs.event(number, half)
 
+    tile_events((0, 1, 2, 3))
     arrivals((0, 1, 4))
+    tile_events((4, 5, 6))
     for ref, index in weights:
         swap(ref, index).wait_recv()
     select(other_w, 1 - k)
     arrivals((2, 3))
+    tile_events(range(7, 15))
     siblings((0, 1, 2, 5))
     multiply(0)
     arrivals((5, 8, 10))
     siblings((3, 6, 9, 11))
     multiply(1)
     join(0)
+    jj[col] = tiles[...].reshape(512, 128).astype(F32).T[0:64].astype(BF16)
+    corner = ColumnGather(jj, jj_send, jj_recv, pos)
+    corner.begin()
     arrivals((6, 7, 9))
     siblings((4, 7, 8, 10))
     multiply(2)
     join(1)
+    corner.middle()
     arrivals((11, 12, 13, 14))
 
     fetch_rows.wait()
@@ -489,12 +522,11 @@
     cr[col] = cov_cols[...].T[0:64].astype(BF16)
     cov_events((0, 1))
     finish(0)
+    join(3)
     cov_events((2, 3, 4))
-    join(3)
     finish(1)
-    cov_events((5, 6))
     finish(2)
-    cov_events((7, 8, 9))
+    corner.end()
     finish(3)
     raw = total[...]
     mass = jnp.sum(raw * raw, axis=0, keepdims=True)
@@ -514,10 +546,7 @@
     kc[x, y] = own_keys
     keys = PlaneGather(kc, 128, kc_send, kc_recv, pos)
     keys.begin()
-    cov_events((10, 11, 12, 13, 14))
-    jj[col] = cc[:, :, :, 0:128].reshape(512, 128).astype(F32).T[0:64].astype(BF16)
-    corner = ColumnGather(jj, jj_send, jj_recv, pos)
-    corner.begin()
+    cov_events((5, 6, 9))
     for _, into in y_copies:
         into.wait_recv()
     sum_x[x] = sum_y[0] + sum_y[1] + sum_y[2] + sum_y[3]
@@ -594,7 +623,7 @@
         relay(number + 1)
 
     panel_rows = ColumnGather(cr, cr_send, cr_recv, pos)
-    corner.middle()
+    cov_events((7, 8))
     relay(0)
     key_event(0)
     for _, into in c_copies:
@@ -605,11 +634,12 @@
     scale = lax.rsqrt(mass / HIDDEN + EPSILON) * (1.0 / 32.0)
     scale_ref[...] = scale * scale
     first_keys.middle()
-    corner.end()
+    cov_events((10, 11, 12))
     key_event(1)
     first_keys.end()
     panel_rows.begin()
     key_event(2)
+    cov_events((13, 14))
 
     def save(number, source, target):
         return pltpu.make_async_copy(source, target, out_sem.at[16 + number])
@@ -664,6 +694,7 @@
     panel_rows.finish()
     first_keys.finish()
     corner.finish()
+    corner_tiles.finish()
     save(4, kr, kr_out).start()
     for ref, index in weights:
         swap(ref, index).wait_send()
@@ -685,7 +716,7 @@
     save(4, kr, kr_out).wait()
 
 
-def panel(subject, gain, w_gate, w_up, cov):
+def panel(residual, positions, gain, w_gate, w_up, cov):
     dma = pltpu.SemaphoreType.DMA
     vmem = pl.BlockSpec(memory_space=pltpu.VMEM)
     anywhere = pl.BlockSpec(memory_space=pl.ANY)
@@ -701,7 +732,7 @@
         name="keys_and_panel",
         out_shape=tuple(jax.ShapeDtypeStruct(*one) for one in spread)
         + (jax.ShapeDtypeStruct((512, 512), F32), jax.ShapeDtypeStruct((8, PROMPTS), F32)),
-        in_specs=[vmem] * 2 + [anywhere] * 3,
+        in_specs=[vmem] * 3 + [anywhere] * 3,
         out_specs=(anywhere,) * 5 + (vmem,) * 2,
         scratch_shapes=[
             pltpu.VMEM(*spread[0]), pltpu.VMEM(*spread[1]), pltpu.VMEM(*spread[2]), pltpu.VMEM(*spread[2]),
@@ -724,16 +755,21 @@
             pltpu.VMEM((8, 8, PROMPTS), F32),
             pltpu.VMEM((64, 2048), F32),
             pltpu.VMEM((1024, 128), F32),
-            dma((4,)), dma((2,)), dma((2,)), dma((7,)), dma((7,)), dma((2, 16)), dma((2, 16)), dma((2, 16)), dma((2, 16)),
+            pltpu.VMEM((64, 128), F32),
+            pltpu.VMEM((2, 4, 64, 128), BF16),
+            dma((5,)), dma((2,)), dma((2,)), dma((7,)), dma((7,)), dma((2, 16)), dma((2, 16)), dma((2, 16)), dma((2, 16)),
             dma((4, 6)), dma((4, 6)), dma((3,)), dma((3,)), dma((3,)), dma((3,)), dma((7,)), dma((7,)), dma((2, 16)), dma((2, 16)),
             dma((2, 16)), dma((2, 16)), dma((8,)), dma((8,)), dma((8,)), dma((8,)), dma((8,)), dma((8,)), dma((2, 16)), dma((2, 16)),
-            dma((16, 4)), dma((16, 4)), dma((21,)),
+            dma((16, 4)), dma((16, 4)), dma((21,)), dma((2, 16)), dma((2, 16)),
         ],
         compiler_params=pltpu.CompilerParams(collective_id=0, has_side_effects=True, vmem_limit_bytes=VMEM_LIMIT),
-    )(subject, gain, w_gate, w_up, cov)
-
-
-def update_kernel(cov_ref, kc_ref, kr_ref, k5_ref, cr_ref, cc_ref, inv_ref, scale_ref, out_ref, covb, outb, panel, in_sem, out_sem):
+    )(residual, positions, gain, w_gate, w_up, cov)
+
+
+def update_kernel(
+    cov_ref, kc_ref, cc_ref, kr_ref, k5_ref, cr_ref, inv_ref, scale_ref, out_ref,
+    covb, kcb, ccb, outb, panel, weights, rows, cov_sem, kc_sem, cc_sem, out_sem, zeros, zero_sem,
+):
     x, y, z, k = here()
     row = x * 4 + y
     col = z * 2 + k
@@ -742,75 +778,94 @@
     tn = (((0,), (0,)), ((), ()))
     dot = functools.partial(lax.dot_general, preferred_element_type=F32)
 
-    def load(step):
+    def load_cov(step):
         area = (pl.ds(step * 128, 1024 - step * 128), pl.ds(step * 256, 256))
-        return pltpu.make_async_copy(cov_ref.at[area], covb.at[step % 2, pl.ds(step * 128, 1024 - step * 128)], in_sem.at[step % 2])
+        return pltpu.make_async_copy(cov_ref.at[area], covb.at[area], cov_sem.at[step])
+
+    def load_kc(step):
+        area = pl.ds(step * 2, 2)
+        return pltpu.make_async_copy(kc_ref.at[area], kcb.at[area], kc_sem.at[step])
+
+    def load_cc(step):
+        area = (slice(None), slice(None), pl.ds(step * 256, 256))
+        return pltpu.make_async_copy(cc_ref.at[area], ccb.at[area], cc_sem.at[step])
 
     def store(step):
-        return pltpu.make_async_copy(outb.at[step % 2], out_ref.at[:, pl.ds(step * 256, 256)], out_sem.at[step % 2])
-
-    load(0).start()
-    load(1).start()
+        top = step * 128
+        source = outb.at[step % 2, pl.ds(top, 1024 - top)]
+        return pltpu.make_async_copy(source, out_ref.at[pl.ds(top, 1024 - top), pl.ds(step * 256, 256)], out_sem.at[step % 2])
+
+    def clear(step):
+        top = step * 128
+        return pltpu.make_async_copy(zeros.at[pl.ds(0, top)], out_ref.at[pl.ds(0, top), pl.ds(step * 256, 256)], zero_sem.at[step])
+
+    for step in range(8):
+        load_kc(step).start()
+        load_cc(step).start()
+        load_cov(step).start()
+    zeros[...] = jnp.zeros_like(zeros)
+    for step in range(1, 8):
+        clear(step).start()
     inverse = inv_ref[...]
     inverse_high = inverse.astype(BF16)
     first = k5_ref[...].reshape(512, PROMPTS)
     raw_rows = kr_ref[...].reshape(1024, PROMPTS)
-    rows = (raw_rows.astype(F32) * scale_ref[0:1]).astype(BF16)
     matrix_rows = cr_ref[...].reshape(512, 1024).astype(F32) + dot(first, raw_rows, nt)
     high, low = split(matrix_rows)
-    panel[...] = dot(inverse_high, high, nn)
-    own = inv_ref[pl.ds(pl.multiple_of(col * 64, 64), 64), :]
-    own_high, own_low = split(own)
-    own_panel = dot(own_high, high, nn) + (dot(own_low, high, nn) + dot(own_high, low, nn))
-    panel_low = panel[...].astype(BF16)
+    panel_rows = dot(inverse_high, high, nn).astype(BF16)
+    weights[...] = dot(panel_rows, inverse_high, tn).astype(BF16)
+    own_high, own_low = split(inv_ref[pl.ds(pl.multiple_of(col * 64, 64), 64), :])
+    panel[...] = dot(own_high, high, nn) + (dot(own_low, high, nn) + dot(own_high, low, nn))
+    rows[...] = (raw_rows.astype(F32) * scale_ref[0:1] - dot(weights[...], first, nn)).astype(BF16)
     for step in range(8):
         top = step * 128
         height = 1024 - top
-        load(step).wait()
+        load_kc(step).wait()
+        load_cc(step).wait()
+        load_cov(step).wait()
         if step >= 2:
             store(step - 2).wait()
-        cols = kc_ref[2 * step : 2 * step + 2].reshape(256, PROMPTS)
-        matrix_cols = cc_ref[:, :, step * 256 : (step + 1) * 256].reshape(512, 256).astype(F32) + dot(first, cols, nt)
-        panel_cols = dot(inverse_high, matrix_cols.astype(BF16), nn).astype(BF16)
-        value = covb[step % 2, top:1024] + dot(rows[top:], cols, nt) - dot(panel_low[:, top:], panel_cols, tn)
+        cols = kcb[2 * step : 2 * step + 2].reshape(256, PROMPTS)
+        panel_cols = ccb[:, :, step * 256 : (step + 1) * 256].reshape(512, 256)
+        value = covb[top:1024, step * 256 : (step + 1) * 256] + (dot(rows[top:], cols, nt) - dot(weights[top:], panel_cols, nn))
         if step == 0:
-            value = jnp.concatenate([own_panel.T, value[:, 64:]], axis=1)
-        i = lax.broadcasted_iota(jnp.int32, (height, 256), 0) + top
-        j = lax.broadcasted_iota(jnp.int32, (height, 256), 1) + step * 256
+            value = jnp.concatenate([panel[...].T, value[:, 64:]], axis=1)
+        edge = min(256, height)
+        i = lax.broadcasted_iota(jnp.int32, (edge, 256), 0) + top
+        j = lax.broadcasted_iota(jnp.int32, (edge, 256), 1) + step * 256
         row_global = (i // 64 * 16 + row) * 64 + i % 64
         col_global = (j // 64 * 8 + col) * 64 + j % 64
-        outb[step % 2, top:1024] = jnp.where(row_global >= col_global, value, 0.0)
-        if step:
-            outb[step % 2, 0:top] = jnp.zeros((top, 256), F32)
+        outb[step % 2, top : top + edge] = jnp.where(row_global >= col_global, value[:edge], 0.0)
+        if edge < height:
+            outb[step % 2, top + edge : 1024] = value[edge:]
         store(step).start()
-        if step + 2 < 8:
-            load(step + 2).start()
     store(6).wait()
     store(7).wait()
+    for step in range(1, 8):
+        clear(step).wait()
 
 
 def update(cov, kc, kr, k5, cr, cc, inverse, scale):
     dma = pltpu.SemaphoreType.DMA
     vmem = pl.BlockSpec(memory_space=pltpu.VMEM)
+    anywhere = pl.BlockSpec(memory_space=pl.ANY)
     return pl.pallas_call(
         update_kernel,
         name="update_lower",
         out_shape=jax.ShapeDtypeStruct((1024, 2048), F32),
-        in_specs=[pl.BlockSpec(memory_space=pl.ANY)] + [vmem] * 7,
-        out_specs=pl.BlockSpec(memory_space=pl.ANY),
+        in_specs=[anywhere] * 3 + [vmem] * 5,
+        out_specs=anywhere,
         scratch_shapes=[
-            pltpu.VMEM((2, 1024, 256), F32), pltpu.VMEM((2, 1024, 256), F32), pltpu.VMEM((512, 1024), F32), dma((2,)), dma((2,)),
+            pltpu.VMEM((1024, 2048), F32), pltpu.VMEM((16, 128, PROMPTS), BF16), pltpu.VMEM((8, 64, 2048), BF16),
+            pltpu.VMEM((2, 1024, 256), F32), pltpu.VMEM((64, 1024), F32), pltpu.VMEM((1024, 512), BF16), pltpu.VMEM((1024, PROMPTS), BF16),
+            dma((8,)), dma((8,)), dma((8,)), dma((2,)), pltpu.VMEM((896, 256), F32), dma((8,)),
         ],
         compiler_params=pltpu.CompilerParams(vmem_limit_bytes=VMEM_LIMIT),
-    )(cov, kc, kr, k5, cr, cc, inverse, scale)
+    )(cov, kc, cc, kr, k5, cr, inverse, scale)
 
 
 def on_device(residual, positions, norm_gain, w_gate, w_up, covariance):
-    prompts, tokens, _ = residual.shape
-    token = lax.broadcasted_iota(jnp.int32, (prompts, tokens), 1)
-    picked = jnp.where((token == positions[:, None])[:, :, None], residual, jnp.zeros_like(residual))
-    subject = jnp.sum(picked.astype(F32), axis=1).astype(BF16)
-    kc, kr, k5, cr, cc, inverse, scale = panel(subject, norm_gain[None, :], w_gate, w_up, covariance)
+    kc, kr, k5, cr, cc, inverse, scale = panel(residual, positions, norm_gain, w_gate, w_up, covariance)
     kc = kc.reshape(16, 128, PROMPTS)
     kr = kr.reshape(16, 64, PROMPTS)
     cc = cc.reshape(8, 64, 2048)

time: 150 us -> 146 us (0.973)
  other arithmetic: 3.25 us -> 0 us
    pallas_call x1, Pallas kernels: 124 us -> 132 us  [panel(): pl.pallas_call(panel_kernel, name='keys_and_panel', out_shape=tuple((jax....]
    pallas_call x1, Pallas kernels: 20.6 us -> 14.6 us  [update(): pl.pallas_call(update_kernel, name='update_lower', out_shape=jax.ShapeDty...]
    reduce_sum x1 -> x0, other arithmetic: 2.52 us -> none  [on_device(): subject = jnp.sum(picked.astype(F32), axis=1).astype(BF16)]
where the time goes in v4:
time: 146 us
  Pallas kernels  146 us (100%)
    pallas_call x1, Pallas kernels, panel(): pl.pallas_call(panel_kernel, name='keys_and_panel', out_shape=tuple((jax....  132 us
    pallas_call x1, Pallas kernels, update(): pl.pallas_call(update_kernel, name='update_lower', out_shape=jax.ShapeDty...  14.6 us

profile of v4, /device:TPU:20, one launch (start us, length us, event | category | flops | bytes accessed | tf_op | source)
XLA Modules:
  0.0 146.4 jit_solution(12877463551367085829)
XLA Ops:
  0.0 131.6 %keys_and_panel.1 = (bf16[4,4,128,1024]{3,2,1,0:T(8,128)(2,1)}, bf16[4,4,64,1024]{3,2,1,0:T(8,128)(2,1)}, bf16[8,64,1024]{2,1,0:T(8,128)(2,1)}, bf16[8,64,1024]{...) custom-call(bf16[64,16,640]{2,1,0:T(8,128)(2,1)} %residual_ref.1, ...), custom_call_target="tpu_custom_call" | custom-call | tf_op jit(solution)/shard_map/keys_and_panel/pallas_call | solution.py:730
  131.6 14.6 %update_lower.1 = f32[1024,2048]{1,0:T(8,128)} custom-call(f32[1024,2048]{1,0:T(8,128)} %cov_ref.3, bf16[16,128,1024]{2,1,0:T(8,128)(2,1)} %bitcast.3, bf16[8,64,2048]{2,1,0:T(8,128)(2,1)} %bitcast.5, bf16[16,64,1024]{2,1,0:T(8,128)(2,1)} %bitcast.4, bf16[8,64,1024]{2,1,0:T(8,128)(2,1)} %get-tuple-element.15.k5_ref, ...), custom_call_target="tpu_custom_call" | custom-call | tf_op jit(solution)/shard_map/update_lower/pallas_call | solution.py:852

commit v5 on v4

--- a/solution.py
+++ b/solution.py
@@ -357,21 +357,19 @@
 
     def select(source, core):
         def body(step, carry):
-            for index in range(2):
-                low = source[index, :, pl.ds(pl.multiple_of(step * 128, 128), 128)]
-                high = source[index, :, pl.ds(pl.multiple_of(512 + step * 128, 128), 128)]
+            first = pl.ds(pl.multiple_of(step * 128, 128), 128)
+            second = pl.ds(pl.multiple_of(512 + step * 128, 128), 128)
+            rows = pl.ds(pl.multiple_of(core * 640, 128), 640)
+            for index, lanes in enumerate((first, second)):
+                gate, up = source[0, :, lanes], source[1, :, lanes]
 
                 @pl.when(k == 0)
                 def _():
-                    sel_w[step, pl.ds(pl.multiple_of(core * 640, 128), 640), pl.ds(index * 128, 128)] = jnp.concatenate(
-                        [low[:, :64], high[:, :64]], axis=1
-                    )
+                    sel_w[step, rows, pl.ds(index * 128, 128)] = jnp.concatenate([gate[:, :64], up[:, :64]], axis=1)
 
                 @pl.when(k == 1)
                 def _():
-                    sel_w[step, pl.ds(pl.multiple_of(core * 640, 128), 640), pl.ds(index * 128, 128)] = jnp.concatenate(
-                        [low[:, 64:], high[:, 64:]], axis=1
-                    )
+                    sel_w[step, rows, pl.ds(index * 128, 128)] = jnp.concatenate([gate[:, 64:], up[:, 64:]], axis=1)
 
             return carry
 
@@ -435,47 +433,61 @@
     def dest(step):
         return lax.rem(z + step % 4, 4)
 
-    def hop(chunk, kind):
+    def hop(chunk, kind, tile):
         target = moved(pos, 2, 1 if kind % 2 == 0 else -1)
         return remote(
-            hop_out.at[chunk, kind], hop_in.at[chunk, kind], hop_send.at[chunk, kind], hop_recv.at[chunk, kind], target
+            hop_out.at[chunk, kind, tile], hop_in.at[chunk, kind, tile],
+            hop_send.at[chunk, kind + 6 * tile], hop_recv.at[chunk, kind + 6 * tile], target,
         )
 
-    def send(chunk, kind, value):
-        hop_out[chunk, kind] = value.astype(BF16)
-        hop(chunk, kind).start()
-
-    def multiply(chunk):
+    def lanes(tile):
+        return slice(128 * tile, 128 * tile + 128)
+
+    def multiply(chunk, hold):
+        def send(kind, value):
+            for tile in (0, 1):
+                hop_out[chunk, kind, tile] = value[:, lanes(tile)].astype(BF16)
+                if tile == 0 or not hold:
+                    hop(chunk, kind, tile).start()
+
         value = product(chunk, dest(2))
-        send(chunk, 0, value[:128])
-        send(chunk, 1, value[128:])
+        send(0, value[:128])
+        send(1, value[128:])
         value = product(chunk, dest(1))
-        send(chunk, 2, value[128:])
+        send(2, value[128:])
         part[chunk, 0] = value[:128]
         value = product(chunk, dest(-1))
-        send(chunk, 3, value[:128])
+        send(3, value[:128])
         part[chunk, 1] = value[128:]
         value = product(chunk, dest(0))
         part[chunk, 2] = value[:128]
         part[chunk, 3] = value[128:]
 
-    def join(chunk):
-        hop(chunk, 0).wait_recv()
-        send(chunk, 4, part[chunk, 0] + hop_in[chunk, 0].astype(F32))
-        hop(chunk, 1).wait_recv()
-        send(chunk, 5, part[chunk, 1] + hop_in[chunk, 1].astype(F32))
-
-    def finish(chunk):
+    def release(chunk):
+        for kind in range(4):
+            hop(chunk, kind, 1).start()
+
+    def join(chunk, tile):
+        for kind in (0, 1):
+            hop(chunk, kind, tile).wait_recv()
+            value = part[chunk, kind, :, lanes(tile)] + hop_in[chunk, kind, tile].astype(F32)
+            hop_out[chunk, 4 + kind, tile] = value.astype(BF16)
+            hop(chunk, 4 + kind, tile).start()
+
+    def finish(chunk, tile):
         second = (0, -1, 1, 2)[chunk]
         for half in (0, 1):
             kinds = (4, 3) if half == 0 else (2, 5)
             for kind in kinds:
-                hop(chunk, kind).wait_recv()
-            value = part[chunk, 2 + half] + (hop_in[chunk, kinds[0]].astype(F32) + hop_in[chunk, kinds[1]].astype(F32))
-            gate, up = value[:, :128], value[:, 128:]
+                hop(chunk, kind, tile).wait_recv()
+            value = part[chunk, 2 + half, :, lanes(tile)] + (
+                hop_in[chunk, kinds[0], tile].astype(F32) + hop_in[chunk, kinds[1], tile].astype(F32)
+            )
+            turned = value.T
+            gate, up = turned[:64], turned[64:]
             raw = gate / (1.0 + jnp.exp(-gate)) * up
             place = lax.rem((x if half == 0 else y) + second % 4, 4)
-            total[:, pl.ds(pl.multiple_of(half * 512 + place * 128, 128), 128)] = raw.T
+            total[pl.ds(64 * tile, 64), pl.ds(pl.multiple_of(half * 512 + place * 128, 128), 128)] = raw
 
     covs = PlaneGather(cc, 64, cc_send, cc_recv, pos, only=lambda bx, by: bx < 2)
 
@@ -484,68 +496,85 @@
             for half in (0, 1):
                 covs.event(number, half)
 
-    tile_events((0, 1, 2, 3))
     arrivals((0, 1, 4))
-    tile_events((4, 5, 6))
     for ref, index in weights:
         swap(ref, index).wait_recv()
     select(other_w, 1 - k)
     arrivals((2, 3))
-    tile_events(range(7, 15))
     siblings((0, 1, 2, 5))
-    multiply(0)
+    multiply(0, False)
     arrivals((5, 8, 10))
+    tile_events((0, 1, 2, 3))
     siblings((3, 6, 9, 11))
-    multiply(1)
-    join(0)
+    multiply(1, False)
+    join(0, 0)
+    arrivals((6, 7, 9))
+    tile_events((4, 5, 6, 7, 8))
+    siblings((4, 7, 8, 10))
+    join(0, 1)
+    multiply(2, True)
+    join(1, 0)
+    arrivals((11, 12, 13, 14))
+    fetch_rows.wait()
+
+    @pl.when(x < 2)
+    def _():
+        cc[x, y] = cov_rows[...].astype(BF16)
+
+    siblings((12, 13, 14, 15))
+    multiply(3, True)
+    release(2)
+    release(3)
+    covs.begin()
+    join(2, 0)
+    join(3, 0)
+    join(1, 1)
+    tile_events(range(9, 15))
+    for chunk in range(4):
+        finish(chunk, 0)
+    row = x * 4 + y
+
+    @pl.when(row == 0)
+    def _():
+        first[0, 0] = total[0:64].astype(BF16)
+
+    first_tile = PlaneGather(first, 64, f_send, f_recv, pos, only=lambda bx, by: (bx == 0) & (by == 0))
+    first_tile.begin()
+
+    def first_events(numbers):
+        for number in numbers:
+            first_tile.event(number, 0)
+            first_tile.event(number, 1)
+
+    join(2, 1)
+    join(3, 1)
     jj[col] = tiles[...].reshape(512, 128).astype(F32).T[0:64].astype(BF16)
     corner = ColumnGather(jj, jj_send, jj_recv, pos)
     corner.begin()
-    arrivals((6, 7, 9))
-    siblings((4, 7, 8, 10))
-    multiply(2)
-    join(1)
-    corner.middle()
-    arrivals((11, 12, 13, 14))
-
-    fetch_rows.wait()
-
-    @pl.when(x < 2)
-    def _():
-        cc[x, y] = cov_rows[...].astype(BF16)
-
-    covs.begin()
-    siblings((12, 13, 14, 15))
-    multiply(3)
-    join(2)
     fetch_cols.wait()
     cr[col] = cov_cols[...].T[0:64].astype(BF16)
     cov_events((0, 1))
-    finish(0)
-    join(3)
+    first_events((0, 1, 2, 3))
+    finish(0, 1)
     cov_events((2, 3, 4))
-    finish(1)
-    finish(2)
-    corner.end()
-    finish(3)
+    first_events((4, 5, 6, 7, 8))
+    finish(1, 1)
+    finish(2, 1)
+    corner.middle()
+    finish(3, 1)
     raw = total[...]
     mass = jnp.sum(raw * raw, axis=0, keepdims=True)
-    own_keys = raw.astype(BF16)
-    row = x * 4 + y
-
-    @pl.when(row == 0)
-    def _():
-        first[0, 0] = own_keys[0:64]
-
-    first_tile = PlaneGather(first, 64, f_send, f_recv, pos, only=lambda bx, by: (bx == 0) & (by == 0))
-    first_tile.begin()
     sum_y[y] = jnp.broadcast_to(mass, (8, PROMPTS))
     y_copies = to_axis(sum_y, sy_send, sy_recv, pos, 1)
     for out, _ in y_copies:
         out.start()
-    kc[x, y] = own_keys
+    kc[x, y] = raw.astype(BF16)
     keys = PlaneGather(kc, 128, kc_send, kc_recv, pos)
     keys.begin()
+    first_events(range(9, 15))
+    k5[col] = first[0, 0]
+    first_keys = ColumnGather(k5, k5_send, k5_recv, pos)
+    first_keys.begin()
     cov_events((5, 6, 9))
     for _, into in y_copies:
         into.wait_recv()
@@ -553,23 +582,14 @@
     x_copies = to_axis(sum_x, sx_send, sx_recv, pos, 0)
     for out, _ in x_copies:
         out.start()
-
-    def first_events(numbers):
-        for number in numbers:
-            first_tile.event(number, 0)
-            first_tile.event(number, 1)
-
-    first_events((0, 1, 2, 3))
+    corner.end()
+    first_keys.middle()
     for _, into in x_copies:
         into.wait_recv()
     sum_c[col] = sum_x[0] + sum_x[1] + sum_x[2] + sum_x[3]
     c_copies = to_all_columns(sum_c, sc_send, sc_recv, pos)
     for out, _ in c_copies:
         out.start()
-    first_events(range(4, 15))
-    k5[col] = first[0, 0]
-    first_keys = ColumnGather(k5, k5_send, k5_recv, pos)
-    first_keys.begin()
 
     source = lax.rem(row, 8)
     source_z = source // 2
@@ -626,6 +646,10 @@
     cov_events((7, 8))
     relay(0)
     key_event(0)
+    first_keys.end()
+    key_event(1)
+    cov_events((10, 11))
+    panel_rows.begin()
     for _, into in c_copies:
         into.wait_recv()
     mass = sum_c[0]
@@ -633,13 +657,6 @@
         mass = mass + sum_c[member]
     scale = lax.rsqrt(mass / HIDDEN + EPSILON) * (1.0 / 32.0)
     scale_ref[...] = scale * scale
-    first_keys.middle()
-    cov_events((10, 11, 12))
-    key_event(1)
-    first_keys.end()
-    panel_rows.begin()
-    key_event(2)
-    cov_events((13, 14))
 
     def save(number, source, target):
         return pltpu.make_async_copy(source, target, out_sem.at[16 + number])
@@ -653,15 +670,17 @@
     ).astype(F32)
     k5_scaled[...] = (corner_raw * (scale * scale)[0:1]).astype(BF16).reshape(8, 64, PROMPTS)
     save(0, k5_scaled, k5_out).start()
-    save(1, cc, cc_out).start()
     beside = {
-        3: 0, 4: 1, 5: 3, 6: 5, 7: 7, 8: 9, 9: 11, 10: 13, 11: 15, 12: 17, 13: 19, 14: 21, 15: 23, 16: 24, 17: 25, 18: 26, 19: 28, 20: 30,
+        2: 0, 3: 1, 4: 2, 5: 3, 6: 5, 7: 7, 8: 9, 9: 11, 10: 13, 11: 15, 12: 17, 13: 19, 14: 21, 15: 23, 16: 24, 17: 25, 18: 26, 19: 28, 20: 30,
     }
     extras = [{} for _ in range(4)]
     for number, step in beside.items():
         extras[step // 8][step % 8] = functools.partial(key_event, number)
-    extras[0][2] = panel_rows.middle
-    extras[0][6] = panel_rows.end
+    extras[0][4] = panel_rows.middle
+    extras[1][0] = panel_rows.end
+    extras[0][6] = lambda: cov_events((12,))
+    extras[1][2] = lambda: cov_events((13, 14))
+    extras[1][4] = lambda: save(1, cc, cc_out).start()
     extras[2][6] = lambda: save(2, kc, kc_out).start()
     extras[2][4] = lambda: save(3, cr, cr_out).start()
     factor(aug, work, extras)
@@ -708,7 +727,8 @@
             to_sibling(half, number, *places[number]).wait_send()
     for chunk in range(4):
         for kind in range(6):
-            hop(chunk, kind).wait_send()
+            for tile in (0, 1):
+                hop(chunk, kind, tile).wait_send()
     save(0, k5_scaled, k5_out).wait()
     save(1, cc, cc_out).wait()
     save(2, kc, kc_out).wait()
@@ -747,8 +767,8 @@
             pltpu.VMEM((4, 1280, 256), BF16),
             pltpu.VMEM((8, 64, 128), F32),
             pltpu.VMEM((4, 4, 128, 256), F32),
-            pltpu.VMEM((4, 6, 128, 256), BF16),
-            pltpu.VMEM((4, 6, 128, 256), BF16),
+            pltpu.VMEM((4, 6, 2, 128, 128), BF16),
+            pltpu.VMEM((4, 6, 2, 128, 128), BF16),
             pltpu.VMEM((128, PROMPTS), F32),
             pltpu.VMEM((4, 8, PROMPTS), F32),
             pltpu.VMEM((4, 8, PROMPTS), F32),
@@ -758,7 +778,7 @@
             pltpu.VMEM((64, 128), F32),
             pltpu.VMEM((2, 4, 64, 128), BF16),
             dma((5,)), dma((2,)), dma((2,)), dma((7,)), dma((7,)), dma((2, 16)), dma((2, 16)), dma((2, 16)), dma((2, 16)),
-            dma((4, 6)), dma((4, 6)), dma((3,)), dma((3,)), dma((3,)), dma((3,)), dma((7,)), dma((7,)), dma((2, 16)), dma((2, 16)),
+            dma((4, 12)), dma((4, 12)), dma((3,)), dma((3,)), dma((3,)), dma((3,)), dma((7,)), dma((7,)), dma((2, 16)), dma((2, 16)),
             dma((2, 16)), dma((2, 16)), dma((8,)), dma((8,)), dma((8,)), dma((8,)), dma((8,)), dma((8,)), dma((2, 16)), dma((2, 16)),
             dma((16, 4)), dma((16, 4)), dma((21,)), dma((2, 16)), dma((2, 16)),
         ],

time: 146 us -> 136 us (0.932)
  the two profiles are of different devices: /device:TPU:20 before, /device:TPU:6 now
where the time goes in v5:
time: 136 us
  Pallas kernels  136 us (100%)
    pallas_call x1, Pallas kernels, panel(): pl.pallas_call(panel_kernel, name='keys_and_panel', out_shape=tuple((jax....  121 us
    pallas_call x1, Pallas kernels, update(): pl.pallas_call(update_kernel, name='update_lower', out_shape=jax.ShapeDty...  14.6 us

profile of v5, /device:TPU:6, one launch (start us, length us, event | category | flops | bytes accessed | tf_op | source)
XLA Modules:
  0.0 136.2 jit_solution(17675088161846193170)
XLA Ops:
  0.0 121.4 %keys_and_panel.1 = (bf16[4,4,128,1024]{3,2,1,0:T(8,128)(2,1)}, bf16[4,4,64,1024]{3,2,1,0:T(8,128)(2,1)}, bf16[8,64,1024]{2,1,0:T(8,128)(2,1)}, bf16[8,64,1024]{...) custom-call(bf16[64,16,640]{2,1,0:T(8,128)(2,1)} %residual_ref.1, ...), custom_call_target="tpu_custom_call" | custom-call | tf_op jit(solution)/shard_map/keys_and_panel/pallas_call | solution.py:750
  121.4 14.6 %update_lower.1 = f32[1024,2048]{1,0:T(8,128)} custom-call(f32[1024,2048]{1,0:T(8,128)} %cov_ref.3, bf16[16,128,1024]{2,1,0:T(8,128)(2,1)} %bitcast.3, bf16[8,64,2048]{2,1,0:T(8,128)(2,1)} %bitcast.5, bf16[16,64,1024]{2,1,0:T(8,128)(2,1)} %bitcast.4, bf16[8,64,1024]{2,1,0:T(8,128)(2,1)} %get-tuple-element.15.k5_ref, ...), custom_call_target="tpu_custom_call" | custom-call | tf_op jit(solution)/shard_map/update_lower/pallas_call | solution.py:872

commit v6 on v5

--- a/solution.py
+++ b/solution.py
@@ -29,6 +29,12 @@
     size = 2 if axis == 3 else 4
     place[axis] = lax.rem(place[axis] + (step % size), size)
     return tuple(place)
+
+
+def one_after_other(first, second):
+    if first is not None:
+        first()
+    second()
 
 
 def remote(src, dst, send, recv, target):
@@ -330,7 +336,9 @@
     folded = squared[:, 0:128]
     for group in range(1, 5):
         folded = folded + squared[:, group * 128 : (group + 1) * 128]
-    squares[col] = folded
+    own_mass = jnp.sum(folded, axis=1, keepdims=True)
+    mass_row = jnp.sum(jnp.where(line_of == prompt_of, own_mass, 0.0), axis=0, keepdims=True)
+    squares[col] = jnp.broadcast_to(jnp.concatenate([mass_row, mass_row], axis=1), (8, 128))
     pl.semaphore_wait(barrier, len(peers))
     square_copies = to_all_columns(squares, sq_send, sq_recv, pos)
     for out, _ in square_copies:
@@ -380,7 +388,8 @@
     everyone = squares[0]
     for member in range(1, 8):
         everyone = everyone + squares[member]
-    inverse_rms = lax.rsqrt(jnp.sum(everyone, axis=1, keepdims=True) / WIDTH + EPSILON)
+    everyone = jnp.sum(jnp.where(line_of == prompt_of, everyone[0:1, 0:64], 0.0), axis=1, keepdims=True)
+    inverse_rms = lax.rsqrt(everyone / WIDTH + EPSILON)
     xx[k, x, y] = (subject * inverse_rms * gain_ref[...].reshape(1, 640)).astype(BF16)
 
     gather = PlaneGather(xx.at[k], 64, x_send, x_recv, pos)
@@ -509,27 +518,28 @@
     multiply(1, False)
     join(0, 0)
     arrivals((6, 7, 9))
+    fetch_rows.wait()
+
+    @pl.when(x < 2)
+    def _():
+        cc[x, y] = cov_rows[...].astype(BF16)
+
+    covs.begin()
     tile_events((4, 5, 6, 7, 8))
     siblings((4, 7, 8, 10))
     join(0, 1)
     multiply(2, True)
     join(1, 0)
     arrivals((11, 12, 13, 14))
-    fetch_rows.wait()
-
-    @pl.when(x < 2)
-    def _():
-        cc[x, y] = cov_rows[...].astype(BF16)
-
     siblings((12, 13, 14, 15))
     multiply(3, True)
     release(2)
     release(3)
-    covs.begin()
     join(2, 0)
     join(3, 0)
     join(1, 1)
     tile_events(range(9, 15))
+    cov_events((0, 1))
     for chunk in range(4):
         finish(chunk, 0)
     row = x * 4 + y
@@ -551,12 +561,11 @@
     jj[col] = tiles[...].reshape(512, 128).astype(F32).T[0:64].astype(BF16)
     corner = ColumnGather(jj, jj_send, jj_recv, pos)
     corner.begin()
+    cov_events((2, 3, 4))
     fetch_cols.wait()
     cr[col] = cov_cols[...].T[0:64].astype(BF16)
-    cov_events((0, 1))
     first_events((0, 1, 2, 3))
     finish(0, 1)
-    cov_events((2, 3, 4))
     first_events((4, 5, 6, 7, 8))
     finish(1, 1)
     finish(2, 1)
@@ -648,7 +657,6 @@
     key_event(0)
     first_keys.end()
     key_event(1)
-    cov_events((10, 11))
     panel_rows.begin()
     for _, into in c_copies:
         into.wait_recv()
@@ -671,18 +679,25 @@
     k5_scaled[...] = (corner_raw * (scale * scale)[0:1]).astype(BF16).reshape(8, 64, PROMPTS)
     save(0, k5_scaled, k5_out).start()
     beside = {
-        2: 0, 3: 1, 4: 2, 5: 3, 6: 5, 7: 7, 8: 9, 9: 11, 10: 13, 11: 15, 12: 17, 13: 19, 14: 21, 15: 23, 16: 24, 17: 25, 18: 26, 19: 28, 20: 30,
+        2: 0, 3: 1, 4: 2, 5: 3, 6: 4, 7: 6, 8: 7, 9: 8, 10: 9, 11: 11, 12: 13, 13: 15, 14: 17, 15: 19, 16: 21, 17: 23, 18: 25, 19: 27, 20: 29,
     }
     extras = [{} for _ in range(4)]
     for number, step in beside.items():
         extras[step // 8][step % 8] = functools.partial(key_event, number)
-    extras[0][4] = panel_rows.middle
-    extras[1][0] = panel_rows.end
-    extras[0][6] = lambda: cov_events((12,))
-    extras[1][2] = lambda: cov_events((13, 14))
-    extras[1][4] = lambda: save(1, cc, cc_out).start()
-    extras[2][6] = lambda: save(2, kc, kc_out).start()
-    extras[2][4] = lambda: save(3, cr, cr_out).start()
+    others = (
+        (3, lambda: cov_events((10,))),
+        (4, panel_rows.middle),
+        (6, lambda: cov_events((11,))),
+        (8, panel_rows.end),
+        (8, lambda: cov_events((12,))),
+        (10, lambda: cov_events((13,))),
+        (12, lambda: cov_events((14,))),
+        (14, lambda: save(1, cc, cc_out).start()),
+        (20, lambda: save(3, cr, cr_out).start()),
+        (22, lambda: save(2, kc, kc_out).start()),
+    )
+    for step, action in others:
+        extras[step // 8][step % 8] = functools.partial(one_after_other, extras[step // 8].get(step % 8), action)
     factor(aug, work, extras)
     inv_ref[...] = aug[:, 512:1024]
 
@@ -765,7 +780,7 @@
             pltpu.VMEM((2, 640, 1024), BF16),
             pltpu.VMEM((2, 640, 1024), BF16),
             pltpu.VMEM((4, 1280, 256), BF16),
-            pltpu.VMEM((8, 64, 128), F32),
+            pltpu.VMEM((8, 8, 128), F32),
             pltpu.VMEM((4, 4, 128, 256), F32),
             pltpu.VMEM((4, 6, 2, 128, 128), BF16),
             pltpu.VMEM((4, 6, 2, 128, 128), BF16),

time: 136 us -> 131 us (0.963)
  the two profiles are of different devices: /device:TPU:6 before, /device:TPU:20 now
where the time goes in v6:
time: 131 us; the launch traced here: 130 us
  Pallas kernels  130 us (99%)
    pallas_call x1, Pallas kernels, panel(): pl.pallas_call(panel_kernel, name='keys_and_panel', out_shape=tuple((jax....  115 us
    pallas_call x1, Pallas kernels, update(): pl.pallas_call(update_kernel, name='update_lower', out_shape=jax.ShapeDty...  14.6 us

profile of v6, /device:TPU:20, one launch (start us, length us, event | category | flops | bytes accessed | tf_op | source)
XLA Modules:
  0.0 130.1 jit_solution(13659313082733994688)
XLA Ops:
  0.0 115.3 %keys_and_panel.1 = (bf16[4,4,128,1024]{3,2,1,0:T(8,128)(2,1)}, bf16[4,4,64,1024]{3,2,1,0:T(8,128)(2,1)}, bf16[8,64,1024]{2,1,0:T(8,128)(2,1)}, bf16[8,64,1024]{...) custom-call(bf16[64,16,640]{2,1,0:T(8,128)(2,1)} %residual_ref.1, ...), custom_call_target="tpu_custom_call" | custom-call | tf_op jit(solution)/shard_map/keys_and_panel/pallas_call | solution.py:765
  115.4 14.6 %update_lower.1 = f32[1024,2048]{1,0:T(8,128)} custom-call(f32[1024,2048]{1,0:T(8,128)} %cov_ref.3, bf16[16,128,1024]{2,1,0:T(8,128)(2,1)} %bitcast.3, bf16[8,64,2048]{2,1,0:T(8,128)(2,1)} %bitcast.5, bf16[16,64,1024]{2,1,0:T(8,128)(2,1)} %bitcast.4, bf16[8,64,1024]{2,1,0:T(8,128)(2,1)} %get-tuple-element.15.k5_ref, ...), custom_call_target="tpu_custom_call" | custom-call | tf_op jit(solution)/shard_map/update_lower/pallas_call | solution.py:887

commit v7 on v6

--- a/solution.py
+++ b/solution.py
@@ -98,7 +98,8 @@
     def copy(self, half, kind, first, second, axis, step, part=None):
         axis = axis if half == 0 else 1 - axis
         ref = self.piece(half, first, second, part)
-        return remote(ref, ref, self.send.at[half, kind], self.recv.at[half, kind], moved(self.pos, axis, step))
+        sender = self.send.at[half, kind] if self.only is not None else self.send.at[0 if kind < 4 else 1]
+        return remote(ref, ref, sender, self.recv.at[half, kind], moved(self.pos, axis, step))
 
     def go(self, half, kind):
         first, second, axis, step, part = self.SENT[kind]
@@ -121,6 +122,10 @@
             self.go(half, kind)
 
     def finish(self):
+        if self.only is None:
+            for number, ref in ((0, self.buf.at[0, pl.ds(0, 3)]), (1, self.buf.at[pl.ds(0, 3)])):
+                remote(ref, ref, self.send.at[number], self.recv.at[0, 0], moved(self.pos, 0, 1)).wait_send()
+            return
         for half in (0, 1):
             for kind in range(16):
                 first, second, axis, step, part = self.SENT[kind]
@@ -397,12 +402,12 @@
 
     def to_sibling(half, number, first, second):
         ref = gather.piece(half, first, second)
-        return remote(ref, ref, sib_send.at[half, number], sib_recv.at[half, number], sibling)
+        return remote(ref, ref, sib_send.at[0], sib_recv.at[half, number], sibling)
 
     def from_sibling(half, number, first, second):
         bx, by = gather.block(half, first, second)
         ref = xx.at[1 - k, bx, by, pl.ds(half * 32, 32)]
-        return remote(ref, ref, sib_send.at[half, number], sib_recv.at[half, number], sibling)
+        return remote(ref, ref, sib_send.at[0], sib_recv.at[half, number], sibling)
 
     places = ((0, 0),) + PlaneGather.PLACES
     for half in (0, 1):
@@ -446,7 +451,7 @@
         target = moved(pos, 2, 1 if kind % 2 == 0 else -1)
         return remote(
             hop_out.at[chunk, kind, tile], hop_in.at[chunk, kind, tile],
-            hop_send.at[chunk, kind + 6 * tile], hop_recv.at[chunk, kind + 6 * tile], target,
+            hop_send.at[0], hop_recv.at[chunk, kind + 6 * tile], target,
         )
 
     def lanes(tile):
@@ -737,13 +742,8 @@
             out.wait_send()
     gather.finish()
     covs.finish()
-    for half in (0, 1):
-        for number in range(16):
-            to_sibling(half, number, *places[number]).wait_send()
-    for chunk in range(4):
-        for kind in range(6):
-            for tile in (0, 1):
-                hop(chunk, kind, tile).wait_send()
+    remote(xx.at[k], xx.at[k], sib_send.at[0], sib_recv.at[0, 0], sibling).wait_send()
+    remote(hop_out, hop_in, hop_send.at[0], hop_recv.at[0, 0], sibling).wait_send()
     save(0, k5_scaled, k5_out).wait()
     save(1, cc, cc_out).wait()
     save(2, kc, kc_out).wait()
@@ -792,9 +792,9 @@
             pltpu.VMEM((1024, 128), F32),
             pltpu.VMEM((64, 128), F32),
             pltpu.VMEM((2, 4, 64, 128), BF16),
-            dma((5,)), dma((2,)), dma((2,)), dma((7,)), dma((7,)), dma((2, 16)), dma((2, 16)), dma((2, 16)), dma((2, 16)),
-            dma((4, 12)), dma((4, 12)), dma((3,)), dma((3,)), dma((3,)), dma((3,)), dma((7,)), dma((7,)), dma((2, 16)), dma((2, 16)),
-            dma((2, 16)), dma((2, 16)), dma((8,)), dma((8,)), dma((8,)), dma((8,)), dma((8,)), dma((8,)), dma((2, 16)), dma((2, 16)),
+            dma((5,)), dma((2,)), dma((2,)), dma((7,)), dma((7,)), dma((2,)), dma((2, 16)), dma((1,)), dma((2, 16)),
+            dma((1,)), dma((4, 12)), dma((3,)), dma((3,)), dma((3,)), dma((3,)), dma((7,)), dma((7,)), dma((2, 16)), dma((2, 16)),
+            dma((2,)), dma((2, 16)), dma((8,)), dma((8,)), dma((8,)), dma((8,)), dma((8,)), dma((8,)), dma((2, 16)), dma((2, 16)),
             dma((16, 4)), dma((16, 4)), dma((21,)), dma((2, 16)), dma((2, 16)),
         ],
         compiler_params=pltpu.CompilerParams(collective_id=0, has_side_effects=True, vmem_limit_bytes=VMEM_LIMIT),

time: 131 us -> 130 us (level)
  no operation moved by 1% of the time
where the time goes in v7:
time: 130 us; the launch traced here: 129 us
  Pallas kernels  129 us (99%)
    pallas_call x1, Pallas kernels, panel(): pl.pallas_call(panel_kernel, name='keys_and_panel', out_shape=tuple((jax....  114 us
    pallas_call x1, Pallas kernels, update(): pl.pallas_call(update_kernel, name='update_lower', out_shape=jax.ShapeDty...  14.6 us

profile of v7, /device:TPU:20, one launch (start us, length us, event | category | flops | bytes accessed | tf_op | source)
XLA Modules:
  0.0 128.8 jit_solution(732593153306015815)
XLA Ops:
  0.0 114.1 %keys_and_panel.1 = (bf16[4,4,128,1024]{3,2,1,0:T(8,128)(2,1)}, bf16[4,4,64,1024]{3,2,1,0:T(8,128)(2,1)}, bf16[8,64,1024]{2,1,0:T(8,128)(2,1)}, bf16[8,64,1024]{...) custom-call(bf16[64,16,640]{2,1,0:T(8,128)(2,1)} %residual_ref.1, ...), custom_call_target="tpu_custom_call" | custom-call | tf_op jit(solution)/shard_map/keys_and_panel/pallas_call | solution.py:765
  114.1 14.6 %update_lower.1 = f32[1024,2048]{1,0:T(8,128)} custom-call(f32[1024,2048]{1,0:T(8,128)} %cov_ref.3, bf16[16,128,1024]{2,1,0:T(8,128)(2,1)} %bitcast.3, bf16[8,64,2048]{2,1,0:T(8,128)(2,1)} %bitcast.5, bf16[16,64,1024]{2,1,0:T(8,128)(2,1)} %bitcast.4, bf16[8,64,1024]{2,1,0:T(8,128)(2,1)} %get-tuple-element.15.k5_ref, ...), custom_call_target="tpu_custom_call" | custom-call | tf_op jit(solution)/shard_map/update_lower/pallas_call | solution.py:887

commit v8 on v7

--- a/solution.py
+++ b/solution.py
@@ -17,7 +17,7 @@
 PROMPTS = 1024
 VMEM_LIMIT = 60 * 1024 * 1024
 BASE = 16
-LAG = 2
+LAG = 3
 
 
 def here():
@@ -684,7 +684,7 @@
     k5_scaled[...] = (corner_raw * (scale * scale)[0:1]).astype(BF16).reshape(8, 64, PROMPTS)
     save(0, k5_scaled, k5_out).start()
     beside = {
-        2: 0, 3: 1, 4: 2, 5: 3, 6: 4, 7: 6, 8: 7, 9: 8, 10: 9, 11: 11, 12: 13, 13: 15, 14: 17, 15: 19, 16: 21, 17: 23, 18: 25, 19: 27, 20: 29,
+        2: 0, 3: 1, 4: 2, 5: 3, 6: 4, 7: 6, 8: 7, 9: 8, 10: 9, 11: 11, 12: 13, 13: 15, 14: 17, 15: 18, 16: 19, 17: 20, 18: 21, 19: 22, 20: 23, 21: 25, 22: 27, 23: 29,
     }
     extras = [{} for _ in range(4)]
     for number, step in beside.items():

time: 130 us -> 126 us (0.969)
  Pallas kernels: 129 us -> 124 us
    pallas_call x1, Pallas kernels: 114 us -> 109 us  [panel(): pl.pallas_call(panel_kernel, name='keys_and_panel', out_shape=tuple((jax....]
where the time goes in v8:
time: 126 us; the launch traced here: 124 us
  Pallas kernels  124 us (98%)
    pallas_call x1, Pallas kernels, panel(): pl.pallas_call(panel_kernel, name='keys_and_panel', out_shape=tuple((jax....  109 us
    pallas_call x1, Pallas kernels, update(): pl.pallas_call(update_kernel, name='update_lower', out_shape=jax.ShapeDty...  14.6 us

profile of v8, /device:TPU:20, one launch (start us, length us, event | category | flops | bytes accessed | tf_op | source)
XLA Modules:
  0.0 123.9 jit_solution(11435699578404249511)
XLA Ops:
  0.0 109.2 %keys_and_panel.1 = (bf16[4,4,128,1024]{3,2,1,0:T(8,128)(2,1)}, bf16[4,4,64,1024]{3,2,1,0:T(8,128)(2,1)}, bf16[8,64,1024]{2,1,0:T(8,128)(2,1)}, bf16[8,64,1024]{...) custom-call(bf16[64,16,640]{2,1,0:T(8,128)(2,1)} %residual_ref.1, ...), custom_call_target="tpu_custom_call" | custom-call | tf_op jit(solution)/shard_map/keys_and_panel/pallas_call | solution.py:765
  109.2 14.6 %update_lower.1 = f32[1024,2048]{1,0:T(8,128)} custom-call(f32[1024,2048]{1,0:T(8,128)} %cov_ref.3, bf16[16,128,1024]{2,1,0:T(8,128)(2,1)} %bitcast.3, bf16[8,64,2048]{2,1,0:T(8,128)(2,1)} %bitcast.5, bf16[16,64,1024]{2,1,0:T(8,128)(2,1)} %bitcast.4, bf16[8,64,1024]{2,1,0:T(8,128)(2,1)} %get-tuple-element.15.k5_ref, ...), custom_call_target="tpu_custom_call" | custom-call | tf_op jit(solution)/shard_map/update_lower/pallas_call | solution.py:887

commit v9 on v8

--- a/solution.py
+++ b/solution.py
@@ -17,7 +17,7 @@
 PROMPTS = 1024
 VMEM_LIMIT = 60 * 1024 * 1024
 BASE = 16
-LAG = 3
+LAG = 4
 
 
 def here():
@@ -684,7 +684,7 @@
     k5_scaled[...] = (corner_raw * (scale * scale)[0:1]).astype(BF16).reshape(8, 64, PROMPTS)
     save(0, k5_scaled, k5_out).start()
     beside = {
-        2: 0, 3: 1, 4: 2, 5: 3, 6: 4, 7: 6, 8: 7, 9: 8, 10: 9, 11: 11, 12: 13, 13: 15, 14: 17, 15: 18, 16: 19, 17: 20, 18: 21, 19: 22, 20: 23, 21: 25, 22: 27, 23: 29,
+        2: 0, 3: 1, 4: 2, 5: 3, 6: 4, 7: 6, 8: 7, 9: 8, 10: 9, 11: 11, 12: 13, 13: 15, 14: 17, 15: 18, 16: 19, 17: 20, 18: 21, 19: 22, 20: 23, 21: 24, 22: 25, 23: 26, 24: 27, 25: 28, 26: 29,
     }
     extras = [{} for _ in range(4)]
     for number, step in beside.items():

time: 126 us -> 125 us (level)
  no operation moved by 1% of the time
where the time goes in v9:
time: 125 us; the launch traced here: 123 us
  Pallas kernels  123 us (98%)
    pallas_call x1, Pallas kernels, panel(): pl.pallas_call(panel_kernel, name='keys_and_panel', out_shape=tuple((jax....  109 us
    pallas_call x1, Pallas kernels, update(): pl.pallas_call(update_kernel, name='update_lower', out_shape=jax.ShapeDty...  14.6 us

profile of v9, /device:TPU:20, one launch (start us, length us, event | category | flops | bytes accessed | tf_op | source)
XLA Modules:
  0.0 123.3 jit_solution(4832554289259137499)
XLA Ops:
  0.0 108.6 %keys_and_panel.1 = (bf16[4,4,128,1024]{3,2,1,0:T(8,128)(2,1)}, bf16[4,4,64,1024]{3,2,1,0:T(8,128)(2,1)}, bf16[8,64,1024]{2,1,0:T(8,128)(2,1)}, bf16[8,64,1024]{...) custom-call(bf16[64,16,640]{2,1,0:T(8,128)(2,1)} %residual_ref.1, ...), custom_call_target="tpu_custom_call" | custom-call | tf_op jit(solution)/shard_map/keys_and_panel/pallas_call | solution.py:765
  108.6 14.6 %update_lower.1 = f32[1024,2048]{1,0:T(8,128)} custom-call(f32[1024,2048]{1,0:T(8,128)} %cov_ref.3, bf16[16,128,1024]{2,1,0:T(8,128)(2,1)} %bitcast.3, bf16[8,64,2048]{2,1,0:T(8,128)(2,1)} %bitcast.5, bf16[16,64,1024]{2,1,0:T(8,128)(2,1)} %bitcast.4, bf16[8,64,1024]{2,1,0:T(8,128)(2,1)} %get-tuple-element.15.k5_ref, ...), custom_call_target="tpu_custom_call" | custom-call | tf_op jit(solution)/shard_map/update_lower/pallas_call | solution.py:887
